TPU v7x, 32 devices: a whole 2x2x4 slice. The times are simulated.
32 devices in a mesh: groups: 2 (over y), renv: 16 (over z, x, core).
Axes of the slice: x: 2, y: 2, z: 4, core: 2. Of those that a mesh axis runs over, the one named last changes fastest.
Arguments:
- psi: float32 [256, 16384], P(('groups', 'renv')), parts along dimension 0, may hold values from -18 to 18, as said below
- left_env: float32 [128, 16384], P('groups'), parts along dimension 0, may hold values from -1 to 1.5
- right_env: float32 [512, 16384], P(('groups', 'renv')), parts along dimension 0, may hold values from -1 to 1.5
- send_block: int32 [512, 1], P(('groups', 'renv')), parts along dimension 0, may hold values from 0 to 7
- send_left: int32 [512, 1, 2], P(('groups', 'renv')), parts along dimension 0, may hold values from 0 to 63
- send_live: int32 [512, 1, 2], P(('groups', 'renv')), parts along dimension 0, may hold values from 0 to 1, as said below
- recv_right: int32 [512, 1, 2], P(('groups', 'renv')), parts along dimension 0, may hold values from 0 to 15
- recv_out: int32 [512, 1, 2], P(('groups', 'renv')), parts along dimension 0, may hold values from 0 to 7
- loc_block: int32 [1024], P(('groups', 'renv')), parts along dimension 0, may hold values from 0 to 7
- loc_left: int32 [1024], P(('groups', 'renv')), parts along dimension 0, may hold values from 0 to 63
- loc_right: int32 [1024], P(('groups', 'renv')), parts along dimension 0, may hold values from 0 to 15
Outputs:
- hpsi: float32 [256, 16384], P(('groups', 'renv')), parts along dimension 0
- residual: float32 [256, 16384], P(('groups', 'renv')), parts along dimension 0
There are 2 independent parts, one for each index of `groups`. A program takes and returns all parts, laid end to end along the dimension named above; each array names one. Nothing has to cross between parts.
Inputs may be any that keep to these rules, and one draw needn't show every extreme that they name: psi blocks of owner-ordered index i have entries of size growing with i. `send_live`: in every draw some receiver has every term live from every sender.
All inputs are finite; a program needn't handle non-finite values.
Results may differ from a plain program's by a relative error of at most 0.0003.
Values sent between devices are 32-bit elements; how exact they have to be, the bound alone decides.
No kernel may reach another device: no remote copies, remote signals or barrier semaphores. Data moves between devices by JAX's collectives and lax.ppermute only.
A program may use at most 128 MiB of HBM per device.

v0:
```python
import math

import jax
import jax.numpy as jnp
from jax import lax
from jax.sharding import PartitionSpec as P

HI = lax.Precision.HIGHEST


def place_sum(placed, targets, owned):
    labels = jnp.arange(owned, dtype=jnp.int32)
    onehot = (targets[..., None] == labels).astype(jnp.float32)
    return jnp.einsum("bgn,bgil->nil", onehot, placed, precision=HI)


def shards(
    psi,
    left_env,
    right_env,
    send_block,
    send_left,
    send_live,
    recv_right,
    recv_out,
    loc_block,
    loc_left,
    loc_right,
):
    peers = lax.axis_size("renv")
    owned = psi.shape[0]
    sector = math.isqrt(psi.shape[1])
    psi_mats = psi.reshape(owned, sector, sector)
    left_mats = left_env.reshape(left_env.shape[0], sector, sector)
    right_mats = right_env.reshape(right_env.shape[0], sector, sector)
    slots = send_block.shape[1]
    terms = send_left.shape[2]
    count = peers * slots
    width = math.gcd(count, 16)
    rounds = count // width
    marks = send_live.astype(jnp.float32)
    zeros = jnp.zeros((owned, sector, sector), jnp.float32)
    rights = recv_right.reshape(rounds, width, terms)
    targets = recv_out.reshape(rounds, width, terms)

    def left_batch(items):
        chosen, lindex, weight = items
        moved = jnp.einsum("bgij,bjk->bgik", left_mats[lindex], psi_mats[chosen], precision=HI)
        return moved * weight[..., None, None]

    sent = lax.map(
        left_batch,
        (
            send_block.reshape(rounds, width),
            send_left.reshape(rounds, width, terms),
            marks.reshape(rounds, width, terms),
        ),
    )
    sent = sent.reshape(peers, slots, terms, sector, sector)
    arrived = lax.all_to_all(sent, "renv", split_axis=0, concat_axis=0, tiled=True)
    arrived = arrived.reshape(rounds, width, terms, sector, sector)

    def right_step(total, items):
        moved, rindex, oindex = items
        placed = jnp.einsum("bgik,bgkl->bgil", moved, right_mats[rindex], precision=HI)
        return (total + place_sum(placed, oindex, owned), None)

    hpsi, _ = lax.scan(right_step, zeros, (arrived, rights, targets))
    near = jnp.einsum("kij,kjl->kil", left_mats[loc_left], psi_mats[loc_block], precision=HI)
    near = jnp.einsum("kil,klm->kim", near, right_mats[loc_right], precision=HI)
    labels = jnp.arange(owned, dtype=jnp.int32)
    keep = (loc_block[:, None] == labels).astype(jnp.float32)
    hpsi = hpsi + jnp.einsum("kb,kim->bim", keep, near, precision=HI)
    hpsi = hpsi.reshape(owned, sector * sector)
    correlation, norm = lax.psum((jnp.sum(psi * hpsi), jnp.sum(psi * psi)), "renv")
    theta = correlation / (norm + 1e-06)
    return (hpsi, hpsi - theta * psi)


def solution(mesh):
    placed = (
        P(("groups", "renv"), None),
        P("groups", None),
        P(("groups", "renv"), None),
        P(("groups", "renv"), None),
        P(("groups", "renv"), None, None),
        P(("groups", "renv"), None, None),
        P(("groups", "renv"), None, None),
        P(("groups", "renv"), None, None),
        P(("groups", "renv")),
        P(("groups", "renv")),
        P(("groups", "renv")),
    )
    return jax.shard_map(
        shards,
        mesh=mesh,
        in_specs=placed,
        out_specs=(P(("groups", "renv"), None), P(("groups", "renv"), None)),
        check_vma=False,
    )
```

profile of v0, /device:TPU:0, one launch (start us, length us, event | category | flops | bytes accessed | tf_op | source)
XLA Modules:
  0.0 114.1 jit_solution(535656383293973194)
XLA Ops:
  0.6 0.0 copy-start.2
  0.6 0.0 copy-start.6
  0.7 0.0 copy-start.10
  0.7 0.0 copy-start.7
  0.7 4.9 %copy.27 = f32[8,8,128,128]{3,2,1,0:T(8,128)} copy(f32[8,8,128,128]{3,1,2,0:T(8,128)} %bitcast.63) | data formatting | bytes 8388608
  5.6 0.0 copy-done.2
  5.6 0.1 copy.43
  5.7 0.0 copy-done.6
  5.7 0.1 copy.19
  5.8 0.1 reshape.100
  5.9 0.0 copy-done.10
  5.9 0.0 copy-done.7
  6.0 0.1 copy.20
  6.0 2.9 %gather_fusion = f32[32,128,128]{2,1,0:T(8,128)S(1)} fusion(f32[64,128,128]{2,1,0:T(8,128)} %bitcast.58, s32[1024]{0:T(1024)S(1)} %pad_clamp_fusion.5), kind=kCustom, calls=%fused_computation | custom fusion | bytes 4194432 | tf_op jit(solution)/shard_map/while/body/eval_jaxpr/gather | solution.py:48
  8.9 1.6 %gather_fusion.1 = f32[16,128,128]{2,1,0:T(8,128)} fusion(f32[8,128,128]{2,1,0:T(8,128)S(1)} %bitcast.56, s32[1024]{0:T(1024)S(1)} %pad_clamp_fusion.4), kind=kCustom, calls=%fused_computation.1 | custom fusion | bytes 2097216 | tf_op jit(solution)/shard_map/while/body/eval_jaxpr/gather | solution.py:48
  10.5 4.5 %multiply_bitcast_fusion = f32[16,1,2,128,128]{4,3,2,1,0:T(8,128)} fusion(f32[16,2,128,128]{3,2,1,0:T(8,128)S(1)} %bitcast.61, f32[16,128,128]{2,1,0:T(8,128)} %gather_fusion.1, f32[16,2]{1,0:T(8,128)S(1)} %copy.20), kind=kOutput, calls=%fused_computation.12 | convolution fusion | flops 805830656 | bytes 5243008 | tf_op jit(solution)/shard_map/while/body/eval_jaxpr/bgij,bjk->bgik/dot_general | solution.py:48
  15.0 0.0 copy-start.11
  15.0 7.5 %all-to-all-start = ((f32[16,1,2,128,128]{4,3,2,1,0:T(8,128)}), f32[16,1,2,128,128]{4,3,2,1,0:T(8,128)S(1)}, u32[]{:S(2)}, u32[]{:S(2)}) async-start(f32[16,1,2,128,128]{4,3,2,1,0:T(8,128)} %multiply_bitcast_fusion), calls=%async_computation | async-start | bytes 4194304 | tf_op jit(solution)/shard_map/all_to_all | solution.py:60
  22.5 0.0 copy-done.11
  22.6 0.0 copy-start.9
  22.6 4.2 %gather_fusion.3 = f32[32,128,128]{2,1,0:T(8,128)} fusion(f32[64,128,128]{2,1,0:T(8,128)} %bitcast.59, s32[1024]{0:T(1024)S(1)} %pad_clamp_fusion.2), kind=kCustom, calls=%fused_computation.3 | custom fusion | bytes 4194432 | tf_op jit(solution)/shard_map/gather | solution.py:69
  26.8 0.0 copy-done.9
  26.8 2.0 %gather_fusion.4 = f32[32,128,128]{2,1,0:T(8,128)} fusion(f32[8,128,128]{2,1,0:T(8,128)S(1)} %bitcast.57, s32[1024]{0:T(1024)S(1)} %pad_clamp_fusion.1), kind=kCustom, calls=%fused_computation.4 | custom fusion | bytes 4194432 | tf_op jit(solution)/shard_map/gather | solution.py:69
  28.8 0.0 copy-start.8
  28.8 0.0 copy-start.12
  28.8 1.5 %copy.29 = f32[2,8,128,128]{3,2,1,0:T(8,128)S(1)} copy(f32[2,8,128,128]{3,1,2,0:T(8,128)} %bitcast.64) | data formatting | bytes 2097152
  30.3 0.0 copy-done.8
  30.3 0.1 copy.22
  30.4 0.1 reshape.116
  30.5 0.0 copy-done.12
  30.5 2.0 %gather_fusion.5 = f32[32,128,128]{2,1,0:T(8,128)} fusion(f32[16,128,128]{2,1,0:T(8,128)S(1)} %bitcast.54, s32[1024]{0:T(1024)S(1)} %pad_clamp_fusion), kind=kCustom, calls=%fused_computation.5 | custom fusion | bytes 4194432 | tf_op jit(solution)/shard_map/gather | solution.py:70
  32.6 2.0 %gather_fusion.2 = f32[32,128,128]{2,1,0:T(8,128)} fusion(f32[16,128,128]{2,1,0:T(8,128)S(1)} %bitcast.55, s32[1024]{0:T(1024)S(1)} %pad_clamp_fusion.3), kind=kCustom, calls=%fused_computation.2 | custom fusion | bytes 4194432 | tf_op jit(solution)/shard_map/while/body/eval_jaxpr/gather | solution.py:65
  34.6 0.0 copy-start.1
  34.6 4.6 %fusion.23 = f32[32,128,128]{2,1,0:T(8,128)S(1)} fusion(f32[32,128,128]{2,1,0:T(8,128)} %gather_fusion.3, f32[32,128,128]{2,1,0:T(8,128)} %gather_fusion.4), kind=kOutput, calls=%fused_computation.41 | convolution fusion | flops 805306368 | bytes 6291456 | tf_op jit(solution)/shard_map/kij,kjl->kil/dot_general | solution.py:69
  39.2 0.0 copy-done.1
  39.2 3.5 %fusion.24 = f32[32,128,128]{2,1,0:T(8,128)} fusion(f32[32,128,128]{2,1,0:T(8,128)S(1)} %fusion.23, f32[32,128,128]{2,1,0:T(8,128)S(1)} %copy-done.1), kind=kOutput, calls=%fused_computation.42 | convolution fusion | flops 805306368 | bytes 6291456 | tf_op jit(solution)/shard_map/kil,klm->kim/dot_general | solution.py:70
  42.7 20.9 %all-to-all-done = f32[16,1,2,128,128]{4,3,2,1,0:T(8,128)S(1)} async-done(((f32[16,1,2,128,128]{4,3,2,1,0:T(8,128)}), f32[16,1,2,128,128]{4,3,2,1,0:T(8,128)S(1)}, u32[]{:S(2)}, u32[]{:S(2)}) %all-to-all-start) | async-done | bytes 2097184 | tf_op jit(solution)/shard_map/all_to_all | solution.py:60
  63.7 3.8 %fusion = f32[16,2,128,128]{3,2,1,0:T(8,128)S(1)} fusion(f32[16,2,128,128]{3,2,1,0:T(8,128)} %bitcast.60, f32[16,1,2,128,128]{4,3,2,1,0:T(8,128)S(1)} %all-to-all-done), kind=kOutput, calls=%fused_computation.6 | convolution fusion | flops 805306368 | bytes 6291456 | tf_op jit(solution)/shard_map/while/body/eval_jaxpr/bgik,bgkl->bgil/dot_general | solution.py:65
  67.4 0.0 copy-start
  67.4 0.0 copy-start.3
  67.5 0.0 copy-done.5
  67.5 2.0 %fusion.12 = f32[8,128,128]{2,0,1:T(8,128)S(1)} fusion(f32[16,2,128,128]{3,2,1,0:T(8,128)S(1)} %fusion, s32[16,2]{0,1:T(2,128)S(1)} %bitcast.65), kind=kOutput, calls=%fused_computation.15 | convolution fusion | flops 50331904 | bytes 2621568 | tf_op jit(solution)/shard_map/while/body/eval_jaxpr/bgn,bgil->nil/dot_general | solution.py:14
  69.4 0.0 copy-done
  69.4 0.0 copy-done.3
  69.4 2.6 %multiply_reduce_fusion = (f32[]{:T(128)}, f32[]{:T(128)}, f32[8,16384]{1,0:T(8,128)S(1)}) fusion(f32[8,16384]{1,0:T(8,128)S(1)} %copy-done.3, f32[8,128,128]{2,0,1:T(8,128)S(1)} %fusion.12, f32[32,128,128]{2,1,0:T(8,128)S(1)} %copy-done, s32[32]{0:T(128)S(1)} %copy-done.9), kind=kOutput, calls=%fused_computation.19 | convolution fusion | flops 50987264 | bytes 3670152 | tf_op jit(solution)/shard_map/kb,kim->bim/dot_general | solution.py:73
  72.1 39.9 %all-reduce = (f32[]{:T(128)}, f32[]{:T(128)}) all-reduce(f32[]{:T(128)} %get-tuple-element.30, f32[]{:T(128)} %get-tuple-element.29), channel_id=1, replica_groups=mesh['groups'=2,'renv'=16] {'renv'}, use_global_device_ids=true, to_apply=%region_1.2 | all-reduce | flops 2 | bytes 16 | tf_op jit(solution)/shard_map/psum | solution.py:75
  113.3 0.8 multiply_subtract_fusion
  114.1 0.0 copy-done.4
  (15 shorter events, 0.1 us)
Async XLA Ops:
  0.6 5.0 %copy-start.2 = (f32[8,16384]{1,0:T(8,128)S(1)}, f32[8,16384]{1,0:T(8,128)}, u32[]{:S(2)}) copy-start(f32[8,16384]{1,0:T(8,128)} %param.11) | copy-start | bytes 1572868
  0.6 5.1 %copy-start.6 = (s32[16,1,2]{0,2,1:T(2,128)S(1)}, s32[16,1,2]{0,2,1:T(2,128)}, u32[]{:S(2)}) copy-start(s32[16,1,2]{0,2,1:T(2,128)} %param.15) | copy-start | bytes 388
  0.7 5.3 %copy-start.10 = (s32[16,1]{0,1:T(1,128)S(1)}, s32[16,1]{0,1:T(1,128)}, u32[]{:S(2)}) copy-start(s32[16,1]{0,1:T(1,128)} %param.14) | copy-start | bytes 196
  0.7 5.3 %copy-start.7 = (s32[16,1,2]{0,2,1:T(2,128)S(1)}, s32[16,1,2]{0,2,1:T(2,128)}, u32[]{:S(2)}) copy-start(s32[16,1,2]{0,2,1:T(2,128)} %param.16) | copy-start | bytes 388
  15.0 7.5 %copy-start.11 = (s32[32]{0:T(128)S(1)}, s32[32]{0:T(128)}, u32[]{:S(2)}) copy-start(s32[32]{0:T(128)} %param.20) | copy-start | bytes 388
  15.0 48.6 %all-to-all-start = ((f32[16,1,2,128,128]{4,3,2,1,0:T(8,128)}), f32[16,1,2,128,128]{4,3,2,1,0:T(8,128)S(1)}, u32[]{:S(2)}, u32[]{:S(2)}) async-start(f32[16,1,2,128,128]{4,3,2,1,0:T(8,128)} %multiply_bitcast_fusion), calls=%async_computation | async-start | bytes 4194304 | tf_op jit(solution)/shard_map/all_to_all | solution.py:60
  22.6 4.2 %copy-start.9 = (s32[32]{0:T(128)S(1)}, s32[32]{0:T(128)}, u32[]{:S(2)}) copy-start(s32[32]{0:T(128)} %param.19) | copy-start | bytes 388
  28.8 1.5 %copy-start.8 = (s32[16,1,2]{0,2,1:T(2,128)S(1)}, s32[16,1,2]{0,2,1:T(2,128)}, u32[]{:S(2)}) copy-start(s32[16,1,2]{0,2,1:T(2,128)} %param.17) | copy-start | bytes 388
  28.8 1.7 %copy-start.12 = (s32[32]{0:T(128)S(1)}, s32[32]{0:T(128)}, u32[]{:S(2)}) copy-start(s32[32]{0:T(128)} %param.21) | copy-start | bytes 388
  34.6 4.6 %copy-start.1 = (f32[32,128,128]{2,1,0:T(8,128)S(1)}, f32[32,128,128]{2,1,0:T(8,128)}, u32[]{:S(2)}) copy-start(f32[32,128,128]{2,1,0:T(8,128)} %gather_fusion.5) | copy-start | bytes 6291460
  63.6 3.8 %copy-start.5 = (s32[16,1,2]{0,2,1:T(2,128)S(1)}, s32[16,1,2]{0,2,1:T(2,128)}, u32[]{:S(2)}) copy-start(s32[16,1,2]{0,2,1:T(2,128)} %param.18) | copy-start | bytes 388
  67.4 2.0 %copy-start = (f32[32,128,128]{2,1,0:T(8,128)S(1)}, f32[32,128,128]{2,1,0:T(8,128)}, u32[]{:S(2)}) copy-start(f32[32,128,128]{2,1,0:T(8,128)} %fusion.24) | copy-start | bytes 6291460
  67.4 2.0 %copy-start.3 = (f32[8,16384]{1,0:T(8,128)S(1)}, f32[8,16384]{1,0:T(8,128)}, u32[]{:S(2)}) copy-start(f32[8,16384]{1,0:T(8,128)} %param.11) | copy-start | bytes 1572868
  72.1 42.0 %copy-start.4 = (f32[8,16384]{1,0:T(8,128)}, f32[8,16384]{1,0:T(8,128)S(1)}, u32[]{:S(2)}) copy-start(f32[8,16384]{1,0:T(8,128)S(1)} %get-tuple-element.33) | copy-start | bytes 1572868
where the time goes:
time: 114 us
  blocking collectives  39.9 us (35%)
  local copies, waits for them, and re-layouts  21.7 us (19%)
  matrix products  21 us (18%)
  waiting for transfers between devices  20.9 us (18%)
  starting transfers between devices  7.5 us (7%)
  between operations  2.18 us (2%)
    psum x1, blocking collectives, shards(): lax.psum((jnp.sum(psi * hpsi), jnp.sum(psi * psi)), 'renv')  39.9 us
    all_to_all x1, waiting for transfers between devices, shards(): lax.all_to_all(sent, 'renv', split_axis=0, concat_axis=0, tiled=True)  20.9 us
    all_to_all x1, starting transfers between devices, shards(): lax.all_to_all(sent, 'renv', split_axis=0, concat_axis=0, tiled=True)  7.5 us
    unnamed x29, local copies, waits for them, and re-layouts  6.53 us
    dot_general x1, matrix products, shards(): jnp.einsum('kij,kjl->kil', left_mats[loc_left], psi_mats[loc_block], prec...  4.56 us
    dot_general x1, matrix products, left_batch(): jnp.einsum('bgij,bjk->bgik', left_mats[lindex], psi_mats[chosen], precisi...  4.51 us
    gather x1, local copies, waits for them, and re-layouts, shards(): left_mats[loc_left]  4.23 us
    dot_general x1, matrix products, right_step(): jnp.einsum('bgik,bgkl->bgil', moved, right_mats[rindex], precision=HI)  3.77 us
  transfers between devices with their start and end apart: 1, of which 1 were waited for; matrix products, arithmetic and copies ran while one was open for 18% of the time, Pallas kernels for 0%

commit v1 on v0

v1 whole, which is shorter than its diff:
```python
import math

import jax
import jax.numpy as jnp
from jax import lax
from jax.experimental import pallas as pl
from jax.experimental.pallas import tpu as pltpu
from jax.sharding import PartitionSpec as P

F32 = jnp.float32
BF16 = jnp.bfloat16
SUB = 8
VMEM = pl.BlockSpec(memory_space=pltpu.VMEM)
SMEM = pl.BlockSpec(memory_space=pltpu.SMEM)


def as_rows(blocks, sector):
    count = blocks.shape[0]
    split = blocks.reshape(count // SUB, SUB, sector, sector)
    return split.transpose(0, 2, 1, 3).reshape(count * sector, sector)


def from_rows(rows, count):
    sector = rows.shape[1]
    split = rows.reshape(count // SUB, sector, SUB, sector)
    return split.transpose(0, 2, 1, 3).reshape(count, sector * sector)


def pick(ref, block):
    sector = ref.shape[1]
    start = (block // SUB) * (SUB * sector) + block % SUB
    return ref[pl.ds(start, sector, stride=SUB), :]


def halves(mat):
    high = mat.astype(BF16)
    low = (mat - high.astype(F32)).astype(BF16)
    return jnp.concatenate([high, low], axis=1)


def doubled(mat):
    both = halves(mat)
    return jnp.concatenate([both, both], axis=0)


def product(left, right):
    sector = right.shape[1] // 2
    wide = jnp.dot(left, right, preferred_element_type=F32)
    return wide[:, :sector] + wide[:, sector:]


def gather_kernel(block_ref, psi_ref, out_ref):
    def body(i, carry):
        out_ref[i] = pick(psi_ref, block_ref[i])
        return carry

    lax.fori_loop(0, out_ref.shape[0], body, 0, unroll=4)


def local_kernel(block_ref, left_ref, right_ref, psi_rows, left_rows, right_rows, near_ref, lefts_ref, rights_ref, psis_ref):
    owned = near_ref.shape[0]

    def split_left(i, carry):
        lefts_ref[i] = halves(pick(left_rows, i))
        return carry

    lax.fori_loop(0, lefts_ref.shape[0], split_left, 0, unroll=4)

    def split_right(i, carry):
        rights_ref[i] = doubled(pick(right_rows, i))
        return carry

    lax.fori_loop(0, rights_ref.shape[0], split_right, 0, unroll=4)

    def split_psi(i, carry):
        psis_ref[i] = doubled(pick(psi_rows, i))
        return carry

    lax.fori_loop(0, owned, split_psi, 0, unroll=4)
    near_ref[...] = jnp.zeros_like(near_ref)

    def term(k, carry):
        block = block_ref[k]
        moved = product(lefts_ref[left_ref[k]], psis_ref[block])
        near_ref[block] += product(halves(moved), rights_ref[right_ref[k]])
        return carry

    lax.fori_loop(0, block_ref.shape[0], term, 0, unroll=4)


def remote_kernel(terms, meta_ref, rindex_ref, out_index_ref, came_ref, near_ref, lefts_ref, rights_ref, psi_rows, hpsi_rows, sums_ref, acc):
    count, sector, _ = came_ref.shape
    owned = near_ref.shape[0]
    acc[...] = near_ref[...]

    def block(i, carry):
        weight = doubled(came_ref[i])
        base = i * 2 * terms
        stack = jnp.concatenate([lefts_ref[meta_ref[base + g]] for g in range(terms)], axis=0)
        moved = product(stack, weight)
        for g in range(terms):
            live = meta_ref[base + terms + g].astype(F32)
            one = moved[g * sector : (g + 1) * sector] * live
            acc[out_index_ref[i * terms + g]] += product(halves(one), rights_ref[rindex_ref[i * terms + g]])
        return carry

    lax.fori_loop(0, count, block, 0, unroll=2)
    for b in range(owned):
        start = (b // SUB) * (SUB * sector) + b % SUB
        hpsi_rows[pl.ds(start, sector, stride=SUB), :] = acc[b]
    psi = psi_rows[...]
    corr = jnp.sum(psi * hpsi_rows[...], axis=0, keepdims=True)
    norm = jnp.sum(psi * psi, axis=0, keepdims=True)
    row = lax.broadcasted_iota(jnp.int32, sums_ref.shape, 0)
    sums_ref[...] = jnp.where(row == 0, corr, jnp.where(row == 1, norm, 0.0))


def residual_kernel(sums_ref, hpsi_rows, psi_rows, out_ref):
    total = jnp.sum(sums_ref[...], axis=0)
    whole = jnp.sum(total, axis=1, keepdims=True)
    theta = whole[0:1] / (whole[1:2] + 1e-06)
    out_ref[...] = hpsi_rows[...] - theta * psi_rows[...]


def shards(
    psi,
    left_env,
    right_env,
    send_block,
    send_left,
    send_live,
    recv_right,
    recv_out,
    loc_block,
    loc_left,
    loc_right,
):
    peers = lax.axis_size("renv")
    owned = psi.shape[0]
    sector = math.isqrt(psi.shape[1])
    slots = send_block.shape[1]
    terms = send_left.shape[2]
    count = peers * slots
    lefts = left_env.shape[0]
    rights = right_env.shape[0]
    psi_rows = as_rows(psi, sector)
    left_rows = as_rows(left_env, sector)
    right_rows = as_rows(right_env, sector)
    limit = pltpu.CompilerParams(vmem_limit_bytes=40 * 2**20)

    sent = pl.pallas_call(
        gather_kernel,
        out_shape=jax.ShapeDtypeStruct((count, sector, sector), F32),
        in_specs=[SMEM, VMEM],
        out_specs=VMEM,
        compiler_params=limit,
        name="gather_blocks",
    )(send_block.reshape(count), psi_rows)
    came = lax.all_to_all(sent.reshape(peers, slots, sector, sector), "renv", split_axis=0, concat_axis=0, tiled=True)
    came = came.reshape(count, sector, sector)

    meta = jnp.concatenate([send_left, send_live], axis=2)
    meta = lax.all_to_all(meta, "renv", split_axis=0, concat_axis=0, tiled=True).reshape(count * 2 * terms)

    near, left_parts, right_parts = pl.pallas_call(
        local_kernel,
        out_shape=(
            jax.ShapeDtypeStruct((owned, sector, sector), F32),
            jax.ShapeDtypeStruct((lefts, sector, 2 * sector), BF16),
            jax.ShapeDtypeStruct((rights, 2 * sector, 2 * sector), BF16),
        ),
        in_specs=[SMEM] * 3 + [VMEM] * 3,
        out_specs=(VMEM,) * 3,
        scratch_shapes=[pltpu.VMEM((owned, 2 * sector, 2 * sector), BF16)],
        compiler_params=limit,
        cost_estimate=pl.CostEstimate(flops=2 * 10**9, bytes_accessed=13 * 2**20, transcendentals=0),
        name="local_terms",
    )(loc_block, loc_left, loc_right, psi_rows, left_rows, right_rows)

    hpsi_rows, sums = pl.pallas_call(
        lambda *refs: remote_kernel(terms, *refs),
        out_shape=(
            jax.ShapeDtypeStruct((owned * sector, sector), F32),
            jax.ShapeDtypeStruct((SUB, sector), F32),
        ),
        in_specs=[SMEM] * 3 + [VMEM] * 5,
        out_specs=(VMEM,) * 2,
        scratch_shapes=[pltpu.VMEM((owned, sector, sector), F32)],
        compiler_params=limit,
        name="remote_terms",
    )(meta, recv_right.reshape(-1), recv_out.reshape(-1), came, near, left_parts, right_parts, psi_rows)

    spread = jnp.broadcast_to(sums[None], (peers, SUB, sector))
    sums = lax.all_to_all(spread, "renv", split_axis=0, concat_axis=0, tiled=True)
    residual_rows = pl.pallas_call(
        residual_kernel,
        out_shape=jax.ShapeDtypeStruct((owned * sector, sector), F32),
        in_specs=[VMEM] * 3,
        out_specs=VMEM,
        compiler_params=limit,
        name="residual",
    )(sums, hpsi_rows, psi_rows)
    return (from_rows(hpsi_rows, owned), from_rows(residual_rows, owned))


def solution(mesh):
    placed = (
        P(("groups", "renv"), None),
        P("groups", None),
        P(("groups", "renv"), None),
        P(("groups", "renv"), None),
        P(("groups", "renv"), None, None),
        P(("groups", "renv"), None, None),
        P(("groups", "renv"), None, None),
        P(("groups", "renv"), None, None),
        P(("groups", "renv")),
        P(("groups", "renv")),
        P(("groups", "renv")),
    )
    return jax.shard_map(
        shards,
        mesh=mesh,
        in_specs=placed,
        out_specs=(P(("groups", "renv"), None), P(("groups", "renv"), None)),
        check_vma=False,
    )
```

time: 114 us -> 67.2 us (0.59)
  blocking collectives: 39.9 us -> 13.5 us
  matrix products: 21 us -> 0 us
  waiting for transfers between devices: 20.9 us -> 7.25 us
  Pallas kernels: 0 us -> 13.4 us
  starting transfers between devices: 7.5 us -> 11.1 us
  local copies, waits for them, and re-layouts: 21.7 us -> 19.2 us
  between operations: 2.18 us -> 0.71 us
    psum x1 -> x0, blocking collectives: 39.9 us -> none  [shards(): lax.psum((jnp.sum(psi * hpsi), jnp.sum(psi * psi)), 'renv')]
    dot_general x6 -> x0, matrix products: 21 us -> none  [the longest x1 4.56 us: shards(): jnp.einsum('kij,kjl->kil', left_mats[loc_left], psi_mats[loc_block], prec...]
    gather x6 -> x0, local copies, waits for them, and re-layouts: 14.8 us -> none  [the longest x1 4.23 us: shards(): left_mats[loc_left]]
    all_to_all x1 -> x2, waiting for transfers between devices: 20.9 us -> 7.25 us  [the longest x1 4.47 us: shards(): lax.all_to_all(sent.reshape(peers, slots, sector, sector), 'renv', split_...]
    all_to_all x0 -> x1, blocking collectives: none -> 13.5 us  [shards(): lax.all_to_all(spread, 'renv', split_axis=0, concat_axis=0, tiled=True)]
    pallas_call x0 -> x4, Pallas kernels: none -> 13.4 us  [the longest x1 5.7 us: shards(): pl.pallas_call(local_kernel, out_shape=(jax.ShapeDtypeStruct((owned, sect...]
    unnamed x29 -> x30, local copies, waits for them, and re-layouts: 6.53 us -> 17.8 us
    all_to_all x1 -> x2, starting transfers between devices: 7.5 us -> 11.1 us  [the longest x1 7.36 us: shards(): lax.all_to_all(meta, 'renv', split_axis=0, concat_axis=0, tiled=True)]
  transfers between devices with their start and end apart: 1 -> 2, of which waited for: 1 -> 2; matrix products, arithmetic and copies ran while one was open for 18% -> 4% of each run, Pallas kernels for 0% -> 11%
where the time goes in v1:
time: 67.2 us; the launch traced here: 66.6 us
  local copies, waits for them, and re-layouts  19.2 us (29%)
  blocking collectives  13.5 us (20%)
  Pallas kernels  13.4 us (20%)
  starting transfers between devices  11.1 us (17%)
  waiting for transfers between devices  7.25 us (11%)
  other arithmetic  1.37 us (2%)
  between operations  0.71 us (1%)
    unnamed x30, local copies, waits for them, and re-layouts  17.8 us
    all_to_all x1, blocking collectives, shards(): lax.all_to_all(spread, 'renv', split_axis=0, concat_axis=0, tiled=True)  13.5 us
    all_to_all x1, starting transfers between devices, shards(): lax.all_to_all(meta, 'renv', split_axis=0, concat_axis=0, tiled=True)  7.36 us
    pallas_call x1, Pallas kernels, shards(): pl.pallas_call(local_kernel, out_shape=(jax.ShapeDtypeStruct((owned, sect...  5.7 us
    pallas_call x1, Pallas kernels, shards(): pl.pallas_call(lambda *refs: remote_kernel(terms, *refs), out_shape=(jax....  4.83 us
    all_to_all x1, waiting for transfers between devices, shards(): lax.all_to_all(sent.reshape(peers, slots, sector, sector), 'renv', split_...  4.47 us
    all_to_all x1, starting transfers between devices, shards(): lax.all_to_all(sent.reshape(peers, slots, sector, sector), 'renv', split_...  3.78 us
    all_to_all x1, waiting for transfers between devices, shards(): lax.all_to_all(meta, 'renv', split_axis=0, concat_axis=0, tiled=True)  2.78 us
  transfers between devices with their start and end apart: 2, of which 2 were waited for; matrix products, arithmetic and copies ran while one was open for 4% of the time, Pallas kernels for 11%

profile of v1, /device:TPU:0, one launch (start us, length us, event | category | flops | bytes accessed | tf_op | source)
XLA Modules:
  0.0 66.6 jit_solution(5152636697274891460)
XLA Ops:
  0.6 0.7 %pad_add_fusion = s32[16,1,4]{0,2,1:T(4,128)S(1)} fusion(s32[16,1,2]{0,2,1:T(2,128)} %param.16, s32[16,1,2]{0,2,1:T(2,128)} %param.15), kind=kLoop, calls=%fused_computation | loop fusion | flops 64 | bytes 512 | tf_op jit(solution)/shard_map/concatenate | solution.py:162
  1.3 0.7 %copy.24 = s32[16,1,4]{2,1,0:T(1,128)} copy(s32[16,1,4]{0,2,1:T(4,128)S(1)} %pad_add_fusion) | data formatting | bytes 512 | tf_op jit(solution)/shard_map/concatenate | solution.py:162
  2.0 7.4 %all-to-all-start = ((s32[16,1,4]{2,1,0:T(1,128)}), s32[16,1,4]{2,1,0:T(1,128)S(1)}, u32[]{:S(2)}, u32[]{:S(2)}) async-start(s32[16,1,4]{2,1,0:T(1,128)} %copy.24), calls=%async_computation | async-start | bytes 16384 | tf_op jit(solution)/shard_map/all_to_all | solution.py:163
  9.4 0.0 copy-start
  9.4 1.0 %copy-done = f32[8,16384]{1,0:T(8,128)S(1)} copy-done((f32[8,16384]{1,0:T(8,128)S(1)}, f32[8,16384]{1,0:T(8,128)}, u32[]{:S(2)}) %copy-start) | copy-done | bytes 524312
  10.4 0.0 copy-start.8
  10.4 0.7 copy-done.8
  11.1 1.9 %gather_blocks.1 = f32[16,128,128]{2,1,0:T(8,128)} custom-call(s32[16]{0:T(128)S(1)} %bitcast.40, f32[1024,128]{1,0:T(8,128)S(1)} %bitcast.34), custom_call_target="tpu_custom_call" | custom-call | tf_op jit(solution)/shard_map/gather_blocks/pallas_call | solution.py:151
  12.9 2.8 %all-to-all-done = s32[16,1,4]{2,1,0:T(1,128)S(1)} async-done(((s32[16,1,4]{2,1,0:T(1,128)}), s32[16,1,4]{2,1,0:T(1,128)S(1)}, u32[]{:S(2)}, u32[]{:S(2)}) %all-to-all-start) | async-done | bytes 288 | tf_op jit(solution)/shard_map/all_to_all | solution.py:163
  15.7 0.0 copy-start.2
  15.7 3.8 %all-to-all-start.1 = ((f32[16,1,128,128]{3,2,1,0:T(8,128)}), f32[16,1,128,128]{3,2,1,0:T(8,128)S(1)}, u32[]{:S(2)}, u32[]{:S(2)}) async-start(f32[16,1,128,128]{3,2,1,0:T(8,128)} %bitcast.5), calls=%async_computation.1 | async-start | bytes 2097152 | tf_op jit(solution)/shard_map/all_to_all | solution.py:159
  19.5 0.8 %copy.25 = s32[16,1,2]{2,0,1:T(8,128)S(1)} copy(s32[16,1,2]{0,2,1:T(2,128)} %param.17) | data formatting | bytes 256 | tf_op args[6]
  20.3 0.1 reshape.54.refs_1_
  20.4 0.8 %copy.26 = s32[16,1,2]{2,0,1:T(8,128)S(1)} copy(s32[16,1,2]{0,2,1:T(2,128)} %param.18) | data formatting | bytes 256 | tf_op args[7]
  21.1 0.1 reshape.55.refs_2_
  21.2 0.0 copy-start.1
  21.2 1.0 %copy-done.1 = f32[8,16384]{1,0:T(8,128)S(1)} copy-done((f32[8,16384]{1,0:T(8,128)S(1)}, f32[8,16384]{1,0:T(8,128)}, u32[]{:S(2)}) %copy-start.1) | copy-done | bytes 524312
  22.3 0.0 copy-start.9
  22.3 2.2 %copy-done.9 = f32[64,16384]{1,0:T(8,128)S(1)} copy-done((f32[64,16384]{1,0:T(8,128)S(1)}, f32[64,16384]{1,0:T(8,128)}, u32[]{:S(2)}) %copy-start.9) | copy-done | bytes 4194328
  24.4 0.0 copy-start.10
  24.4 1.2 %copy-done.10 = f32[16,16384]{1,0:T(8,128)S(1)} copy-done((f32[16,16384]{1,0:T(8,128)S(1)}, f32[16,16384]{1,0:T(8,128)}, u32[]{:S(2)}) %copy-start.10) | copy-done | bytes 1048600
  25.7 0.0 copy-start.11
  25.7 0.7 copy-done.11
  26.3 0.0 copy-start.12
  26.3 0.7 copy-done.12
  27.0 0.0 copy-start.13
  27.0 0.7 copy-done.13
  27.6 5.7 %local_terms.1 = (f32[8,128,128]{2,1,0:T(8,128)S(1)}, bf16[64,128,256]{2,1,0:T(8,128)(2,1)S(1)}, bf16[16,256,256]{2,1,0:T(8,128)(2,1)S(1)}) custom-call(s32[32]{0:T(128)S(1)} %copy-done.11, s32[32]{0:T(128)S(1)} %copy-done.12, s32[32]{0:T(128)S(1)} %copy-done.13, f32[1024,128]{1,0:T(8,128)S(1)} %bitcast.35, f32[8192,128]{1,0:T(8,128)S(1)} %bitcast.41, ...), custom_call_target="tpu_custom_call" | custom-call | flops 2000000000 | bytes 13631488 | tf_op jit(solution)/shard_map/local_terms/pallas_call | solution.py:165
  33.3 0.0 copy-start.3
  33.4 2.0 %copy-done.3 = bf16[64,128,256]{2,1,0:T(8,128)(2,1)} copy-done((bf16[64,128,256]{2,1,0:T(8,128)(2,1)}, bf16[64,128,256]{2,1,0:T(8,128)(2,1)S(1)}, u32[]{:S(2)}) %copy-start.3) | copy-done | bytes 4194328
  35.3 0.0 copy-start.5
  35.3 1.3 %copy-done.5 = bf16[16,256,256]{2,1,0:T(8,128)(2,1)} copy-done((bf16[16,256,256]{2,1,0:T(8,128)(2,1)}, bf16[16,256,256]{2,1,0:T(8,128)(2,1)S(1)}, u32[]{:S(2)}) %copy-start.5) | copy-done | bytes 2097176
  36.7 0.5 broadcast.4
  37.2 0.7 %reduce.3 = s32[16,4]{1,0:T(8,128)S(1)} reduce(s32[16,1,4]{2,1,0:T(1,128)S(1)} %all-to-all-done, s32[]{:T(128)} %broadcast.4), dimensions={1}, to_apply=%all_to_all.9.reduce_sub_computation.3 | reduce | bytes 516 | tf_op jit(solution)/shard_map/all_to_all | solution.py:163
  37.8 0.1 reshape.53.refs_0_
  37.9 4.5 %all-to-all-done.1 = f32[16,1,128,128]{3,2,1,0:T(8,128)S(1)} async-done(((f32[16,1,128,128]{3,2,1,0:T(8,128)}), f32[16,1,128,128]{3,2,1,0:T(8,128)S(1)}, u32[]{:S(2)}, u32[]{:S(2)}) %all-to-all-start.1) | async-done | bytes 1048608 | tf_op jit(solution)/shard_map/all_to_all | solution.py:159
  42.4 0.0 copy-done.2
  42.4 0.0 copy-start.4
  42.4 2.2 %copy-done.4 = bf16[64,128,256]{2,1,0:T(8,128)(2,1)S(1)} copy-done((bf16[64,128,256]{2,1,0:T(8,128)(2,1)S(1)}, bf16[64,128,256]{2,1,0:T(8,128)(2,1)}, u32[]{:S(2)}) %copy-start.4) | copy-done | bytes 4194328
  44.6 0.0 copy-start.6
  44.6 1.6 %copy-done.6 = bf16[16,256,256]{2,1,0:T(8,128)(2,1)S(1)} copy-done((bf16[16,256,256]{2,1,0:T(8,128)(2,1)S(1)}, bf16[16,256,256]{2,1,0:T(8,128)(2,1)}, u32[]{:S(2)}) %copy-start.6) | copy-done | bytes 2097176
  46.2 4.8 %remote_terms.1 = (f32[1024,128]{1,0:T(8,128)}, f32[8,128]{1,0:T(8,128)S(1)}) custom-call(s32[64]{0:T(128)S(1)} %reshape.53.refs_0_, s32[32]{0:T(128)S(1)} %reshape.54.refs_1_, s32[32]{0:T(128)S(1)} %reshape.55.refs_2_, f32[16,128,128]{2,1,0:T(8,128)S(1)} %bitcast.38, f32[8,128,128]{2,1,0:T(8,128)S(1)} %get-tuple-element.7.refs_4_, ...), custom_call_target="tpu_custom_call" | custom-call | tf_op jit(solution)/shard_map/remote_terms/pallas_call | solution.py:180
  51.0 13.5 %all_to_all.15.sums_ref = f32[16,8,128]{2,1,0:T(8,128)S(1)} all-to-all(f32[16,8,128]{2,1,0:T(8,128)S(1)} %broadcast_in_dim.2), channel_id=1, replica_groups=mesh['groups'=2,'renv'=16] {'renv'}, dimensions={0} | all-to-all | bytes 131072 | tf_op jit(solution)/shard_map/all_to_all | solution.py:194
  64.5 0.0 copy-start.7
  64.5 1.0 %copy-done.7 = f32[1024,128]{1,0:T(8,128)S(1)} copy-done((f32[1024,128]{1,0:T(8,128)S(1)}, f32[1024,128]{1,0:T(8,128)}, u32[]{:S(2)}) %copy-start.7) | copy-done | bytes 524312
  65.6 1.0 %residual.1 = f32[1024,128]{1,0:T(8,128)} custom-call(f32[16,8,128]{2,1,0:T(8,128)S(1)} %all_to_all.15.sums_ref, f32[1024,128]{1,0:T(8,128)S(1)} %copy-done.7, f32[1024,128]{1,0:T(8,128)S(1)} %bitcast.37), custom_call_target="tpu_custom_call" | custom-call | tf_op jit(solution)/shard_map/residual/pallas_call | solution.py:195
  (1 shorter events, 0.0 us)
Async XLA Ops:
  2.0 13.7 %all-to-all-start = ((s32[16,1,4]{2,1,0:T(1,128)}), s32[16,1,4]{2,1,0:T(1,128)S(1)}, u32[]{:S(2)}, u32[]{:S(2)}) async-start(s32[16,1,4]{2,1,0:T(1,128)} %copy.24), calls=%async_computation | async-start | bytes 16384 | tf_op jit(solution)/shard_map/all_to_all | solution.py:163
  9.4 1.0 %copy-start = (f32[8,16384]{1,0:T(8,128)S(1)}, f32[8,16384]{1,0:T(8,128)}, u32[]{:S(2)}) copy-start(f32[8,16384]{1,0:T(8,128)} %param.11) | copy-start | bytes 1572868
  10.4 0.7 copy-start.8
  15.7 26.7 %copy-start.2 = (f32[8,16384]{1,0:T(8,128)S(1)}, f32[8,16384]{1,0:T(8,128)}, u32[]{:S(2)}) copy-start(f32[8,16384]{1,0:T(8,128)} %param.11) | copy-start | bytes 1572868
  15.7 26.7 %all-to-all-start.1 = ((f32[16,1,128,128]{3,2,1,0:T(8,128)}), f32[16,1,128,128]{3,2,1,0:T(8,128)S(1)}, u32[]{:S(2)}, u32[]{:S(2)}) async-start(f32[16,1,128,128]{3,2,1,0:T(8,128)} %bitcast.5), calls=%async_computation.1 | async-start | bytes 2097152 | tf_op jit(solution)/shard_map/all_to_all | solution.py:159
  21.2 1.0 %copy-start.1 = (f32[8,16384]{1,0:T(8,128)S(1)}, f32[8,16384]{1,0:T(8,128)}, u32[]{:S(2)}) copy-start(f32[8,16384]{1,0:T(8,128)} %param.11) | copy-start | bytes 1572868
  22.3 2.2 %copy-start.9 = (f32[64,16384]{1,0:T(8,128)S(1)}, f32[64,16384]{1,0:T(8,128)}, u32[]{:S(2)}) copy-start(f32[64,16384]{1,0:T(8,128)} %param.12) | copy-start | bytes 12582916
  24.4 1.2 %copy-start.10 = (f32[16,16384]{1,0:T(8,128)S(1)}, f32[16,16384]{1,0:T(8,128)}, u32[]{:S(2)}) copy-start(f32[16,16384]{1,0:T(8,128)} %param.13) | copy-start | bytes 3145732
  25.7 0.7 copy-start.11
  26.3 0.7 copy-start.12
  27.0 0.7 copy-start.13
  33.3 2.0 %copy-start.3 = (bf16[64,128,256]{2,1,0:T(8,128)(2,1)}, bf16[64,128,256]{2,1,0:T(8,128)(2,1)S(1)}, u32[]{:S(2)}) copy-start(bf16[64,128,256]{2,1,0:T(8,128)(2,1)S(1)} %get-tuple-element.8.refs_5_) | copy-start | bytes 12582916
  35.3 1.4 %copy-start.5 = (bf16[16,256,256]{2,1,0:T(8,128)(2,1)}, bf16[16,256,256]{2,1,0:T(8,128)(2,1)S(1)}, u32[]{:S(2)}) copy-start(bf16[16,256,256]{2,1,0:T(8,128)(2,1)S(1)} %get-tuple-element.9.refs_6_) | copy-start | bytes 6291460
  42.4 2.2 %copy-start.4 = (bf16[64,128,256]{2,1,0:T(8,128)(2,1)S(1)}, bf16[64,128,256]{2,1,0:T(8,128)(2,1)}, u32[]{:S(2)}) copy-start(bf16[64,128,256]{2,1,0:T(8,128)(2,1)} %copy-done.3) | copy-start | bytes 12582916
  44.6 1.6 %copy-start.6 = (bf16[16,256,256]{2,1,0:T(8,128)(2,1)S(1)}, bf16[16,256,256]{2,1,0:T(8,128)(2,1)}, u32[]{:S(2)}) copy-start(bf16[16,256,256]{2,1,0:T(8,128)(2,1)} %copy-done.5) | copy-start | bytes 6291460
  64.5 1.0 %copy-start.7 = (f32[1024,128]{1,0:T(8,128)S(1)}, f32[1024,128]{1,0:T(8,128)}, u32[]{:S(2)}) copy-start(f32[1024,128]{1,0:T(8,128)} %get-tuple-element.10.hpsi_rows) | copy-start | bytes 1572868

commit v2 on v1

v2 whole, which is shorter than its diff:
```python
import math

import jax
import jax.numpy as jnp
from jax import lax
from jax.experimental import pallas as pl
from jax.experimental.pallas import tpu as pltpu
from jax.sharding import PartitionSpec as P

F32 = jnp.float32
BF16 = jnp.bfloat16
SUB = 8
VMEM = pl.BlockSpec(memory_space=pltpu.VMEM)
SMEM = pl.BlockSpec(memory_space=pltpu.SMEM)
HBM = pl.BlockSpec(memory_space=pltpu.HBM)


def as_rows(blocks, sector):
    count = blocks.shape[0]
    split = blocks.reshape(count // SUB, SUB, sector, sector)
    return split.transpose(0, 2, 1, 3).reshape(count * sector, sector)


def from_rows(rows, count):
    sector = rows.shape[1]
    split = rows.reshape(count // SUB, sector, SUB, sector)
    return split.transpose(0, 2, 1, 3).reshape(count, sector * sector)


def pick(ref, block):
    sector = ref.shape[1]
    start = (block // SUB) * (SUB * sector) + block % SUB
    return ref[pl.ds(start, sector, stride=SUB), :]


def halves(mat):
    high = mat.astype(BF16)
    low = (mat - high.astype(F32)).astype(BF16)
    return jnp.concatenate([high, low], axis=1)


def doubled(mat):
    both = halves(mat)
    return jnp.concatenate([both, both], axis=0)


def product(left, right):
    sector = right.shape[1] // 2
    wide = jnp.dot(left, right, preferred_element_type=F32)
    return wide[:, :sector] + wide[:, sector:]


def gather_kernel(order, me_ref, block_ref, psi_hbm, *rest):
    outs, (psi_rows, stage, fetch_sem, put_sems) = rest[: len(order)], rest[len(order) :]
    fetch = pltpu.make_async_copy(psi_hbm, psi_rows, fetch_sem)
    fetch.start()
    fetch.wait()
    puts = []
    for i, step in enumerate(order):
        stage[i] = pick(psi_rows, block_ref[peer(me_ref[0], step)])
        put = pltpu.make_async_copy(stage.at[i], outs[i], put_sems.at[i])
        put.start()
        puts.append(put)
    for put in puts:
        put.wait()


def peer(me, step):
    return lax.bitwise_xor(me, step)


def local_kernel(
    terms,
    me_ref,
    send_block_ref,
    send_left_ref,
    send_live_ref,
    rindex_ref,
    out_index_ref,
    block_ref,
    left_ref,
    right_ref,
    psi_rows,
    left_rows,
    right_rows,
    near_ref,
    lefts_hbm,
    rights_hbm,
    lefts_ref,
    rights_ref,
    psis_ref,
    sems,
):
    owned = near_ref.shape[0]

    def split_left(i, carry):
        lefts_ref[i] = halves(pick(left_rows, i))
        return carry

    lax.fori_loop(0, lefts_ref.shape[0], split_left, 0, unroll=4)
    put_left = pltpu.make_async_copy(lefts_ref, lefts_hbm, sems.at[0])
    put_left.start()

    def split_right(i, carry):
        rights_ref[i] = doubled(pick(right_rows, i))
        return carry

    lax.fori_loop(0, rights_ref.shape[0], split_right, 0, unroll=4)
    put_right = pltpu.make_async_copy(rights_ref, rights_hbm, sems.at[1])
    put_right.start()

    def split_psi(i, carry):
        psis_ref[i] = doubled(pick(psi_rows, i))
        return carry

    lax.fori_loop(0, owned, split_psi, 0, unroll=4)
    near_ref[...] = jnp.zeros_like(near_ref)

    def term(k, carry):
        block = block_ref[k]
        moved = product(lefts_ref[left_ref[k]], psis_ref[block])
        near_ref[block] += product(halves(moved), rights_ref[right_ref[k]])
        return carry

    lax.fori_loop(0, block_ref.shape[0], term, 0, unroll=4)
    me = me_ref[0]
    for g in range(terms):
        spot = me * terms + g
        moved = product(lefts_ref[send_left_ref[spot]], psis_ref[send_block_ref[me]])
        moved = moved * send_live_ref[spot].astype(F32)
        near_ref[out_index_ref[spot]] += product(halves(moved), rights_ref[rindex_ref[spot]])
    put_left.wait()
    put_right.wait()


def add_terms(terms, order, me_ref, meta_ref, rindex_ref, out_index_ref, came, lefts_hbm, rights_hbm, acc, lefts_ref, rights_ref, left_sems, right_sems):
    sector = came[0].shape[0]
    senders = [peer(me_ref[0], step) for step in order]
    fetches = []
    for i, sender in enumerate(senders):
        mine = []
        for g in range(terms):
            lindex = meta_ref[sender * 2 * terms + g]
            rindex = rindex_ref[sender * terms + g]
            mine.append(
                pltpu.make_async_copy(
                    lefts_hbm.at[lindex], lefts_ref.at[i, pl.ds(g * sector, sector)], left_sems.at[i, g]
                )
            )
            mine.append(pltpu.make_async_copy(rights_hbm.at[rindex], rights_ref.at[i, g], right_sems.at[i, g]))
        for copy in mine:
            copy.start()
        fetches.append(mine)
    for i, sender in enumerate(senders):
        weight = doubled(came[i][...])
        for copy in fetches[i]:
            copy.wait()
        moved = product(lefts_ref[i], weight)
        for g in range(terms):
            live = meta_ref[sender * 2 * terms + terms + g].astype(F32)
            one = moved[g * sector : (g + 1) * sector] * live
            acc[out_index_ref[sender * terms + g]] += product(halves(one), rights_ref[i, g])


def remote_kernel(terms, order, me_ref, meta_ref, rindex_ref, out_index_ref, *rest):
    came, rest = rest[: len(order)], rest[len(order) :]
    lefts_hbm, rights_hbm, near_ref, acc, lefts_ref, rights_ref, left_sems, right_sems = rest
    acc[...] = near_ref[...]
    add_terms(terms, order, me_ref, meta_ref, rindex_ref, out_index_ref, came, lefts_hbm, rights_hbm, acc, lefts_ref, rights_ref, left_sems, right_sems)


def last_kernel(terms, order, me_ref, meta_ref, rindex_ref, out_index_ref, *rest):
    came, rest = rest[: len(order)], rest[len(order) :]
    lefts_hbm, rights_hbm, near_ref, psi_rows, hpsi_rows, sums_ref, acc, lefts_ref, rights_ref, left_sems, right_sems = rest
    sector = psi_rows.shape[1]
    acc[...] = near_ref[...]
    add_terms(terms, order, me_ref, meta_ref, rindex_ref, out_index_ref, came, lefts_hbm, rights_hbm, acc, lefts_ref, rights_ref, left_sems, right_sems)
    for b in range(acc.shape[0]):
        start = (b // SUB) * (SUB * sector) + b % SUB
        hpsi_rows[pl.ds(start, sector, stride=SUB), :] = acc[b]
    psi = psi_rows[...]
    corr = jnp.sum(psi * hpsi_rows[...], axis=0, keepdims=True)
    norm = jnp.sum(psi * psi, axis=0, keepdims=True)
    row = lax.broadcasted_iota(jnp.int32, sums_ref.shape, 0)
    sums_ref[...] = jnp.where(row == 0, corr, jnp.where(row == 1, norm, 0.0))


def residual_kernel(parts, *refs):
    hpsi_rows, psi_rows, out_ref = refs[parts:]
    total = refs[0][...]
    for part in refs[1:parts]:
        total = total + part[...]
    whole = jnp.sum(total, axis=1, keepdims=True)
    theta = whole[0:1] / (whole[1:2] + 1e-06)
    out_ref[...] = hpsi_rows[...] - theta * psi_rows[...]


def exchange(value, steps, peers):
    return [lax.ppermute(value, "renv", [(s, s ^ step) for s in range(peers)]) for step in steps]


def shards(
    psi,
    left_env,
    right_env,
    send_block,
    send_left,
    send_live,
    recv_right,
    recv_out,
    loc_block,
    loc_left,
    loc_right,
):
    peers = lax.axis_size("renv")
    owned = psi.shape[0]
    sector = math.isqrt(psi.shape[1])
    terms = send_left.shape[2]
    lefts = left_env.shape[0]
    rights = right_env.shape[0]
    psi_rows = as_rows(psi, sector)
    left_rows = as_rows(left_env, sector)
    right_rows = as_rows(right_env, sector)
    limit = pltpu.CompilerParams(vmem_limit_bytes=32 * 2**20)
    me = lax.axis_index("renv").astype(jnp.int32).reshape(1)
    mat = jax.ShapeDtypeStruct((sector, sector), F32)
    order = list(range(peers - 1, 0, -1))

    sent = pl.pallas_call(
        lambda *refs: gather_kernel(order, *refs),
        out_shape=[mat] * len(order),
        in_specs=[SMEM, SMEM, HBM],
        out_specs=[HBM] * len(order),
        scratch_shapes=[
            pltpu.VMEM(psi_rows.shape, F32),
            pltpu.VMEM((len(order), sector, sector), F32),
            pltpu.SemaphoreType.DMA,
            pltpu.SemaphoreType.DMA((len(order),)),
        ],
        compiler_params=limit,
        name="gather_blocks",
    )(me, send_block.reshape(-1), psi_rows)
    came = [lax.ppermute(block, "renv", [(s, s ^ step) for s in range(peers)]) for block, step in zip(sent, order)]

    meta = jnp.concatenate([send_left, send_live], axis=2).reshape(-1)
    every = lax.all_gather(meta, "renv")
    meta = lax.dynamic_slice_in_dim(every, me[0] * (2 * terms), 2 * terms, axis=1).reshape(-1)

    near, left_parts, right_parts = pl.pallas_call(
        lambda *refs: local_kernel(terms, *refs),
        out_shape=(
            jax.ShapeDtypeStruct((owned, sector, sector), F32),
            jax.ShapeDtypeStruct((lefts, sector, 2 * sector), BF16),
            jax.ShapeDtypeStruct((rights, 2 * sector, 2 * sector), BF16),
        ),
        in_specs=[SMEM] * 9 + [VMEM] * 3,
        out_specs=(VMEM, HBM, HBM),
        scratch_shapes=[
            pltpu.VMEM((lefts, sector, 2 * sector), BF16),
            pltpu.VMEM((rights, 2 * sector, 2 * sector), BF16),
            pltpu.VMEM((owned, 2 * sector, 2 * sector), BF16),
            pltpu.SemaphoreType.DMA((2,)),
        ],
        compiler_params=limit,
        cost_estimate=pl.CostEstimate(flops=2 * 10**9, bytes_accessed=13 * 2**20, transcendentals=0),
        name="local_terms",
    )(
        me,
        send_block.reshape(-1),
        send_left.reshape(-1),
        send_live.reshape(-1),
        recv_right.reshape(-1),
        recv_out.reshape(-1),
        loc_block,
        loc_left,
        loc_right,
        psi_rows,
        left_rows,
        right_rows,
    )

    width = 4
    groups = [(order[i : i + width], came[i : i + width]) for i in range(0, len(order), width)]
    groups.reverse()
    for number, (steps, blocks) in enumerate(groups):
        last = number == len(groups) - 1
        size = len(steps)
        scratch = [
            pltpu.VMEM((size, terms * sector, 2 * sector), BF16),
            pltpu.VMEM((size, terms, 2 * sector, 2 * sector), BF16),
            pltpu.SemaphoreType.DMA((size, terms)),
            pltpu.SemaphoreType.DMA((size, terms)),
        ]
        total = jax.ShapeDtypeStruct(near.shape, F32)
        operands = (me, meta, recv_right.reshape(-1), recv_out.reshape(-1), *blocks, left_parts, right_parts, near)
        specs = [SMEM] * 4 + [VMEM] * size + [HBM] * 2 + [VMEM]
        if not last:
            near = pl.pallas_call(
                lambda *refs, steps=steps: remote_kernel(terms, steps, *refs),
                out_shape=total,
                in_specs=specs,
                out_specs=VMEM,
                scratch_shapes=scratch,
                compiler_params=limit,
                cost_estimate=pl.CostEstimate(flops=2 * 10**8, bytes_accessed=4 * 2**20, transcendentals=0),
                name="remote_terms",
            )(*operands)
        else:
            hpsi_rows, sums = pl.pallas_call(
                lambda *refs, steps=steps: last_kernel(terms, steps, *refs),
                out_shape=(
                    jax.ShapeDtypeStruct((owned * sector, sector), F32),
                    jax.ShapeDtypeStruct((SUB, sector), F32),
                ),
                in_specs=specs + [VMEM],
                out_specs=(VMEM,) * 2,
                scratch_shapes=[pltpu.VMEM(near.shape, F32)] + scratch,
                compiler_params=limit,
                name="last_terms",
            )(*operands, psi_rows)

    stride = 1
    parts = [sums]
    while stride < peers:
        radix = min(4, peers // stride)
        if stride > 1:
            sums = sum(parts[1:], parts[0])
        parts = [sums] + exchange(sums, [digit * stride for digit in range(1, radix)], peers)
        stride *= radix
    residual_rows = pl.pallas_call(
        lambda *refs: residual_kernel(len(parts), *refs),
        out_shape=jax.ShapeDtypeStruct((owned * sector, sector), F32),
        in_specs=[VMEM] * (len(parts) + 2),
        out_specs=VMEM,
        compiler_params=limit,
        name="residual",
    )(*parts, hpsi_rows, psi_rows)
    return (from_rows(hpsi_rows, owned), from_rows(residual_rows, owned))


def solution(mesh):
    placed = (
        P(("groups", "renv"), None),
        P("groups", None),
        P(("groups", "renv"), None),
        P(("groups", "renv"), None),
        P(("groups", "renv"), None, None),
        P(("groups", "renv"), None, None),
        P(("groups", "renv"), None, None),
        P(("groups", "renv"), None, None),
        P(("groups", "renv")),
        P(("groups", "renv")),
        P(("groups", "renv")),
    )
    return jax.shard_map(
        shards,
        mesh=mesh,
        in_specs=placed,
        out_specs=(P(("groups", "renv"), None), P(("groups", "renv"), None)),
        check_vma=False,
    )
```

time: 67.2 us -> 101 us (1.50)
  starting transfers between devices: 11.1 us -> 28.2 us
  Pallas kernels: 13.4 us -> 27 us
  blocking collectives: 13.5 us -> 20.7 us
  waiting for transfers between devices: 7.25 us -> 3.38 us
    ppermute x0 -> x21, starting transfers between devices: none -> 28.2 us  [the longest x15 21.7 us: shards(): lax.ppermute(block, 'renv', [(s, s ^ step) for s in range(peers)])]
    all_gather x0 -> x1, blocking collectives: none -> 20.7 us  [shards(): every = lax.all_gather(meta, 'renv')]
    pallas_call x4 -> x7, Pallas kernels: 13.4 us -> 27 us  [the longest x3 11.9 us: shards(): pl.pallas_call(lambda *refs, steps=steps: remote_kernel(terms, steps, *re...]
    all_to_all x1 -> x0, blocking collectives: 13.5 us -> none  [shards(): lax.all_to_all(spread, 'renv', split_axis=0, concat_axis=0, tiled=True)]
    all_to_all x2 -> x0, starting transfers between devices: 11.1 us -> none  [the longest x1 7.36 us: shards(): lax.all_to_all(meta, 'renv', split_axis=0, concat_axis=0, tiled=True)]
    all_to_all x2 -> x0, waiting for transfers between devices: 7.25 us -> none  [the longest x1 4.47 us: shards(): lax.all_to_all(sent.reshape(peers, slots, sector, sector), 'renv', split_...]
    ppermute x0 -> x21, waiting for transfers between devices: none -> 3.38 us  [the longest x6 3.34 us: exchange(): lax.ppermute(value, 'renv', [(s, s ^ step) for s in range(peers)])]
    unnamed x30 -> x37, local copies, waits for them, and re-layouts: 17.8 us -> 17.7 us
  transfers between devices with their start and end apart: 2 -> 21, of which waited for: 2 -> 4; matrix products, arithmetic and copies ran while one was open for 4% -> 7% of each run, Pallas kernels for 11% -> 18%
where the time goes in v2:
time: 101 us
  starting transfers between devices  28.2 us (28%)
  Pallas kernels  27 us (27%)
  blocking collectives  20.7 us (20%)
  local copies, waits for them, and re-layouts  20.2 us (20%)
  waiting for transfers between devices  3.38 us (3%)
    ppermute x15, starting transfers between devices, shards(): lax.ppermute(block, 'renv', [(s, s ^ step) for s in range(peers)])  21.7 us
    all_gather x1, blocking collectives, shards(): every = lax.all_gather(meta, 'renv')  20.7 us
    unnamed x37, local copies, waits for them, and re-layouts  17.7 us
    pallas_call x3, Pallas kernels, shards(): pl.pallas_call(lambda *refs, steps=steps: remote_kernel(terms, steps, *re...  11.9 us
    pallas_call x1, Pallas kernels, shards(): pl.pallas_call(lambda *refs: local_kernel(terms, *refs), out_shape=(jax.S...  6.53 us
    ppermute x6, starting transfers between devices, exchange(): lax.ppermute(value, 'renv', [(s, s ^ step) for s in range(peers)])  6.44 us
    pallas_call x1, Pallas kernels, shards(): pl.pallas_call(lambda *refs, steps=steps: last_kernel(terms, steps, *refs...  5.1 us
    ppermute x6, waiting for transfers between devices, exchange(): lax.ppermute(value, 'renv', [(s, s ^ step) for s in range(peers)])  3.34 us
  transfers between devices with their start and end apart: 21, of which 4 were waited for; matrix products, arithmetic and copies ran while one was open for 7% of the time, Pallas kernels for 18%

profile of v2, /device:TPU:0, one launch (start us, length us, event | category | flops | bytes accessed | tf_op | source)
XLA Modules:
  0.0 100.9 jit_solution(3777667020651723515)
XLA Ops:
  0.7 1.0 %copy-done.3 = f32[8,16384]{1,0:T(8,128)S(1)} copy-done((f32[8,16384]{1,0:T(8,128)S(1)}, f32[8,16384]{1,0:T(8,128)}, u32[]{:S(2)}) %copy-start.3) | copy-done | bytes 524312
  1.7 0.7 copy-done.7
  2.4 2.5 %gather_blocks.1 = (f32[128,128]{1,0:T(8,128)}, f32[128,128]{1,0:T(8,128)}, f32[128,128]{1,0:T(8,128)}, f32[128,128]{1,0:T(8,128)}, f32[128,128]{1,0:T(8,128)S(1...) custom-call(s32[1]{0:T(128)} %bitcast.refs_0_, ...), custom_call_target="tpu_custom_call" | custom-call | tf_op jit(solution)/shard_map/gather_blocks/pallas_call | solution.py:229
  4.8 4.5 %collective-permute-start.4 = (f32[128,128]{1,0:T(8,128)S(1)}, f32[128,128]{1,0:T(8,128)S(1)}, u32[]{:S(2)}, u32[]{:S(2)}) collective-permute-start(f32[128,128]{1,0:T(8,128)S(1)} %get-tuple-element.28), channel_id=1, source_target_pairs={{0,11},{1,10},{2,9},{3,8},{4,15},{5,14},{6,13},{7,12},{8,3},{9,2},... | collective-permute-start | bytes 196616 | tf_op jit(solution)/shard_map/ppermute | solution.py:243
  9.3 0.6 collective-permute-start.5
  9.9 2.3 %collective-permute-start.6 = (f32[128,128]{1,0:T(8,128)S(1)}, f32[128,128]{1,0:T(8,128)S(1)}, u32[]{:S(2)}, u32[]{:S(2)}) collective-permute-start(f32[128,128]{1,0:T(8,128)S(1)} %get-tuple-element.30), channel_id=1, source_target_pairs={{0,9},{1,8},{2,11},{3,10},{4,13},{5,12},{6,15},{7,14},{8,1},{9,0},... | collective-permute-start | bytes 196616 | tf_op jit(solution)/shard_map/ppermute | solution.py:243
  12.2 2.2 %collective-permute-start.8 = (f32[128,128]{1,0:T(8,128)S(1)}, f32[128,128]{1,0:T(8,128)S(1)}, u32[]{:S(2)}, u32[]{:S(2)}) collective-permute-start(f32[128,128]{1,0:T(8,128)S(1)} %get-tuple-element.32), channel_id=1, source_target_pairs={{0,7},{1,6},{2,5},{3,4},{4,3},{5,2},{6,1},{7,0},{8,15},{9,14},{10,... | collective-permute-start | bytes 196616 | tf_op jit(solution)/shard_map/ppermute | solution.py:243
  14.8 0.8 copy.24
  15.7 0.8 copy.25
  16.5 0.8 copy.26
  17.4 0.8 copy.27
  18.2 1.4 %collective-permute-start.10 = (f32[128,128]{1,0:T(8,128)S(1)}, f32[128,128]{1,0:T(8,128)S(1)}, u32[]{:S(2)}, u32[]{:S(2)}) collective-permute-start(f32[128,128]{1,0:T(8,128)S(1)} %get-tuple-element.34), channel_id=1, source_target_pairs={{0,5},{1,4},{2,7},{3,6},{4,1},{5,0},{6,3},{7,2},{8,13},{9,12},{10,... | collective-permute-start | bytes 196616 | tf_op jit(solution)/shard_map/ppermute | solution.py:243
  19.6 0.5 collective-permute-start.11
  20.1 1.2 %collective-permute-start.12 = (f32[128,128]{1,0:T(8,128)}, f32[128,128]{1,0:T(8,128)S(1)}, u32[]{:S(2)}, u32[]{:S(2)}) collective-permute-start(f32[128,128]{1,0:T(8,128)} %get-tuple-element.36), channel_id=1, source_target_pairs={{0,3},{1,2},{2,1},{3,0},{4,7},{5,6},{6,5},{7,4},{8,11},{9,10},{10,... | collective-permute-start | bytes 196616 | tf_op jit(solution)/shard_map/ppermute | solution.py:243
  21.3 0.5 collective-permute-start.13
  22.0 1.0 %copy-done.4 = f32[8,16384]{1,0:T(8,128)S(1)} copy-done((f32[8,16384]{1,0:T(8,128)S(1)}, f32[8,16384]{1,0:T(8,128)}, u32[]{:S(2)}) %copy-start.4) | copy-done | bytes 524312
  23.0 0.7 copy-done.8
  23.7 2.2 %copy-done.9 = f32[64,16384]{1,0:T(8,128)S(1)} copy-done((f32[64,16384]{1,0:T(8,128)S(1)}, f32[64,16384]{1,0:T(8,128)}, u32[]{:S(2)}) %copy-start.9) | copy-done | bytes 4194328
  25.9 1.2 %copy-done.10 = f32[16,16384]{1,0:T(8,128)S(1)} copy-done((f32[16,16384]{1,0:T(8,128)S(1)}, f32[16,16384]{1,0:T(8,128)}, u32[]{:S(2)}) %copy-start.10) | copy-done | bytes 1048600
  27.1 0.7 copy-done.11
  27.7 0.7 copy-done.12
  28.4 0.7 copy-done.13
  29.0 6.5 %local_terms.1 = (f32[8,128,128]{2,1,0:T(8,128)S(1)}, bf16[64,128,256]{2,1,0:T(8,128)(2,1)S(1)}, bf16[16,256,256]{2,1,0:T(8,128)(2,1)S(1)}) custom-call(s32[1]{0:T(128)} %bitcast.refs_0_, s32[16]{0:T(128)S(1)} %bitcast.43, s32[32]{0:T(128)S(1)} %reshape.71.refs_2_, s32[32]{0:T(128)S(1)} %reshape.72.refs_3_, s32[32]{0:T(128)S(1)} %reshape.66.refs_4_.refs_2_, ...), custom_call_target="tpu_custom_call" | custom-call | flops 2000000000 | bytes 13631488 | tf_op jit(solution)/shard_map/local_terms/pallas_call | solution.py:249
  35.6 2.0 %copy-done = bf16[64,128,256]{2,1,0:T(8,128)(2,1)} copy-done((bf16[64,128,256]{2,1,0:T(8,128)(2,1)}, bf16[64,128,256]{2,1,0:T(8,128)(2,1)S(1)}, u32[]{:S(2)}) %copy-start) | copy-done | bytes 4194328
  37.6 3.7 %collective-permute-start = (f32[128,128]{1,0:T(8,128)}, f32[128,128]{1,0:T(8,128)S(1)}, u32[]{:S(2)}, u32[]{:S(2)}) collective-permute-start(f32[128,128]{1,0:T(8,128)} %get-tuple-element.22), channel_id=1, source_target_pairs={{0,15},{1,14},{2,13},{3,12},{4,11},{5,10},{6,9},{7,8},{8,7},{9,6},... | collective-permute-start | bytes 196616 | tf_op jit(solution)/shard_map/ppermute | solution.py:243
  41.3 1.0 collective-permute-start.1
  42.2 2.6 %collective-permute-start.2 = (f32[128,128]{1,0:T(8,128)}, f32[128,128]{1,0:T(8,128)S(1)}, u32[]{:S(2)}, u32[]{:S(2)}) collective-permute-start(f32[128,128]{1,0:T(8,128)} %get-tuple-element.24), channel_id=1, source_target_pairs={{0,13},{1,12},{2,15},{3,14},{4,9},{5,8},{6,11},{7,10},{8,5},{9,4},... | collective-permute-start | bytes 196616 | tf_op jit(solution)/shard_map/ppermute | solution.py:243
  44.8 0.8 collective-permute-start.3
  45.6 0.6 pad_add_fusion
  46.2 0.7 copy.23
  46.9 0.7 reshape.81
  47.6 20.7 %all-gather = s32[16,1,64]{2,1,0:T(1,128)S(1)} all-gather(s32[1,1,64]{2,1,0:T(1,128)} %reshape.81), channel_id=1, replica_groups=mesh['groups'=2,'renv'=16] {'renv'}, dimensions={0}, use_global_device_ids=true | all-gather | bytes 4352 | tf_op jit(solution)/shard_map/all_gather | solution.py:246
  68.2 0.7 dynamic-slice_reduce_fusion
  68.9 0.8 reshape.65.refs_1_
  69.7 2.2 %copy-done.1 = bf16[64,128,256]{2,1,0:T(8,128)(2,1)S(1)} copy-done((bf16[64,128,256]{2,1,0:T(8,128)(2,1)S(1)}, bf16[64,128,256]{2,1,0:T(8,128)(2,1)}, u32[]{:S(2)}) %copy-start.1) | copy-done | bytes 4194328
  71.9 3.3 %remote_terms.3.refs_10_ = f32[8,128,128]{2,1,0:T(8,128)S(1)} custom-call(s32[1]{0:T(128)} %bitcast.refs_0_, s32[64]{0:T(128)S(1)} %reshape.65.refs_1_, s32[32]{0:T(128)S(1)} %reshape.66.refs_4_.refs_2_, s32[32]{0:T(128)S(1)} %reshape.67.refs_5_.refs_3_, f32[128,128]{1,0:T(8,128)S(1)} %collective-permute-done.12.refs_4_, ...), custom_call_target="tpu_custom_call" | custom-call | flops 200000000 | bytes 4194304 | tf_op jit(solution)/shard_map/remote_terms/pallas_call | solution.py:298
  75.2 4.2 %remote_terms.4.refs_10_ = f32[8,128,128]{2,1,0:T(8,128)S(1)} custom-call(s32[1]{0:T(128)} %bitcast.refs_0_, s32[64]{0:T(128)S(1)} %reshape.65.refs_1_, s32[32]{0:T(128)S(1)} %reshape.66.refs_4_.refs_2_, s32[32]{0:T(128)S(1)} %reshape.67.refs_5_.refs_3_, f32[128,128]{1,0:T(8,128)S(1)} %collective-permute-done.8.refs_4_, ...), custom_call_target="tpu_custom_call" | custom-call | flops 200000000 | bytes 4194304 | tf_op jit(solution)/shard_map/remote_terms/pallas_call | solution.py:298
  79.4 4.5 %remote_terms.5.refs_10_ = f32[8,128,128]{2,1,0:T(8,128)S(1)} custom-call(s32[1]{0:T(128)} %bitcast.refs_0_, s32[64]{0:T(128)S(1)} %reshape.65.refs_1_, s32[32]{0:T(128)S(1)} %reshape.66.refs_4_.refs_2_, s32[32]{0:T(128)S(1)} %reshape.67.refs_5_.refs_3_, f32[128,128]{1,0:T(8,128)S(1)} %collective-permute-done.4.refs_4_, ...), custom_call_target="tpu_custom_call" | custom-call | flops 200000000 | bytes 4194304 | tf_op jit(solution)/shard_map/remote_terms/pallas_call | solution.py:298
  83.9 5.1 %last_terms.1 = (f32[1024,128]{1,0:T(8,128)}, f32[8,128]{1,0:T(8,128)S(1)}) custom-call(s32[1]{0:T(128)} %bitcast.refs_0_, s32[64]{0:T(128)S(1)} %reshape.65.refs_1_, s32[32]{0:T(128)S(1)} %reshape.66.refs_4_.refs_2_, s32[32]{0:T(128)S(1)} %reshape.67.refs_5_.refs_3_, f32[128,128]{1,0:T(8,128)S(1)} %collective-permute-done.refs_4_, ...), custom_call_target="tpu_custom_call" | custom-call | tf_op jit(solution)/shard_map/last_terms/pallas_call | solution.py:309
  89.1 1.9 %collective-permute-start.16 = (f32[8,128]{1,0:T(8,128)S(1)}, f32[8,128]{1,0:T(8,128)S(1)}, u32[]{:S(2)}, u32[]{:S(2)}) collective-permute-start(f32[8,128]{1,0:T(8,128)S(1)} %get-tuple-element.41), channel_id=1, source_target_pairs={{0,2},{1,3},{2,0},{3,1},{4,6},{5,7},{6,4},{7,5},{8,10},{9,11},{10,... | collective-permute-start | bytes 12296 | tf_op jit(solution)/shard_map/ppermute | solution.py:199
  91.1 1.1 %collective-permute-done.17 = f32[8,128]{1,0:T(8,128)S(1)} collective-permute-done((f32[8,128]{1,0:T(8,128)S(1)}, f32[8,128]{1,0:T(8,128)S(1)}, u32[]{:S(2)}, u32[]{:S(2)}) %collective-permute-start.17) | collective-permute-done | bytes 4128 | tf_op jit(solution)/shard_map/ppermute | solution.py:199
  92.2 0.6 collective-permute-done.16
  92.9 0.5 collective-permute-start.19
  93.4 3.9 %collective-permute-start.18 = (f32[8,128]{1,0:T(8,128)S(1)}, f32[8,128]{1,0:T(8,128)S(1)}, u32[]{:S(2)}, u32[]{:S(2)}) collective-permute-start(f32[8,128]{1,0:T(8,128)S(1)} %add_add_fusion.refs_0_), channel_id=1, source_target_pairs={{0,4},{1,5},{2,6},{3,7},{4,0},{5,1},{6,2},{7,3},{8,12},{9,13},{10,... | collective-permute-start | bytes 12296 | tf_op jit(solution)/shard_map/ppermute | solution.py:199
  97.3 1.0 %collective-permute-done.20.refs_3_ = f32[8,128]{1,0:T(8,128)S(1)} collective-permute-done((f32[8,128]{1,0:T(8,128)S(1)}, f32[8,128]{1,0:T(8,128)S(1)}, u32[]{:S(2)}, u32[]{:S(2)}) %collective-permute-start.20) | collective-permute-done | bytes 4128 | tf_op jit(solution)/shard_map/ppermute | solution.py:199
  98.3 0.6 collective-permute-done.18.refs_1_
  98.9 1.0 %copy-done.6 = f32[1024,128]{1,0:T(8,128)S(1)} copy-done((f32[1024,128]{1,0:T(8,128)S(1)}, f32[1024,128]{1,0:T(8,128)}, u32[]{:S(2)}) %copy-start.6) | copy-done | bytes 524312
  99.9 1.0 residual.1
  (48 shorter events, 1.2 us)
Async XLA Ops:
  0.6 44.9 %copy-start.15 = (s32[16,1,2]{0,2,1:T(2,128)S(1)}, s32[16,1,2]{0,2,1:T(2,128)}, u32[]{:S(2)}) copy-start(s32[16,1,2]{0,2,1:T(2,128)} %param.15) | copy-start | bytes 388
  0.6 44.9 %copy-start.14 = (s32[16,1,2]{0,2,1:T(2,128)S(1)}, s32[16,1,2]{0,2,1:T(2,128)}, u32[]{:S(2)}) copy-start(s32[16,1,2]{0,2,1:T(2,128)} %param.16) | copy-start | bytes 388
  0.7 1.0 %copy-start.3 = (f32[8,16384]{1,0:T(8,128)S(1)}, f32[8,16384]{1,0:T(8,128)}, u32[]{:S(2)}) copy-start(f32[8,16384]{1,0:T(8,128)} %param.11) | copy-start | bytes 1572868
  1.7 0.7 copy-start.7
  4.8 13.4 %collective-permute-start.4 = (f32[128,128]{1,0:T(8,128)S(1)}, f32[128,128]{1,0:T(8,128)S(1)}, u32[]{:S(2)}, u32[]{:S(2)}) collective-permute-start(f32[128,128]{1,0:T(8,128)S(1)} %get-tuple-element.28), channel_id=1, source_target_pairs={{0,11},{1,10},{2,9},{3,8},{4,15},{5,14},{6,13},{7,12},{8,3},{9,2},... | collective-permute-start | bytes 196616 | tf_op jit(solution)/shard_map/ppermute | solution.py:243
  9.3 10.4 %collective-permute-start.5 = (f32[128,128]{1,0:T(8,128)S(1)}, f32[128,128]{1,0:T(8,128)S(1)}, u32[]{:S(2)}, u32[]{:S(2)}) collective-permute-start(f32[128,128]{1,0:T(8,128)S(1)} %get-tuple-element.29), channel_id=1, source_target_pairs={{0,10},{1,11},{2,8},{3,9},{4,14},{5,15},{6,12},{7,13},{8,2},{9,3},... | collective-permute-start | bytes 196616 | tf_op jit(solution)/shard_map/ppermute | solution.py:243
  9.9 10.2 %collective-permute-start.6 = (f32[128,128]{1,0:T(8,128)S(1)}, f32[128,128]{1,0:T(8,128)S(1)}, u32[]{:S(2)}, u32[]{:S(2)}) collective-permute-start(f32[128,128]{1,0:T(8,128)S(1)} %get-tuple-element.30), channel_id=1, source_target_pairs={{0,9},{1,8},{2,11},{3,10},{4,13},{5,12},{6,15},{7,14},{8,1},{9,0},... | collective-permute-start | bytes 196616 | tf_op jit(solution)/shard_map/ppermute | solution.py:243
  12.2 9.0 %collective-permute-start.8 = (f32[128,128]{1,0:T(8,128)S(1)}, f32[128,128]{1,0:T(8,128)S(1)}, u32[]{:S(2)}, u32[]{:S(2)}) collective-permute-start(f32[128,128]{1,0:T(8,128)S(1)} %get-tuple-element.32), channel_id=1, source_target_pairs={{0,7},{1,6},{2,5},{3,4},{4,3},{5,2},{6,1},{7,0},{8,15},{9,14},{10,... | collective-permute-start | bytes 196616 | tf_op jit(solution)/shard_map/ppermute | solution.py:243
  14.4 7.4 %collective-permute-start.9 = (f32[128,128]{1,0:T(8,128)S(1)}, f32[128,128]{1,0:T(8,128)S(1)}, u32[]{:S(2)}, u32[]{:S(2)}) collective-permute-start(f32[128,128]{1,0:T(8,128)S(1)} %get-tuple-element.33), channel_id=1, source_target_pairs={{0,6},{1,7},{2,4},{3,5},{4,2},{5,3},{6,0},{7,1},{8,14},{9,15},{10,... | collective-permute-start | bytes 196616 | tf_op jit(solution)/shard_map/ppermute | solution.py:243
  18.2 19.3 %collective-permute-start.10 = (f32[128,128]{1,0:T(8,128)S(1)}, f32[128,128]{1,0:T(8,128)S(1)}, u32[]{:S(2)}, u32[]{:S(2)}) collective-permute-start(f32[128,128]{1,0:T(8,128)S(1)} %get-tuple-element.34), channel_id=1, source_target_pairs={{0,5},{1,4},{2,7},{3,6},{4,1},{5,0},{6,3},{7,2},{8,13},{9,12},{10,... | collective-permute-start | bytes 196616 | tf_op jit(solution)/shard_map/ppermute | solution.py:243
  19.6 21.6 %collective-permute-start.11 = (f32[128,128]{1,0:T(8,128)S(1)}, f32[128,128]{1,0:T(8,128)S(1)}, u32[]{:S(2)}, u32[]{:S(2)}) collective-permute-start(f32[128,128]{1,0:T(8,128)S(1)} %get-tuple-element.35), channel_id=1, source_target_pairs={{0,4},{1,5},{2,6},{3,7},{4,0},{5,1},{6,2},{7,3},{8,12},{9,13},{10,... | collective-permute-start | bytes 196616 | tf_op jit(solution)/shard_map/ppermute | solution.py:243
  20.1 22.1 %collective-permute-start.12 = (f32[128,128]{1,0:T(8,128)}, f32[128,128]{1,0:T(8,128)S(1)}, u32[]{:S(2)}, u32[]{:S(2)}) collective-permute-start(f32[128,128]{1,0:T(8,128)} %get-tuple-element.36), channel_id=1, source_target_pairs={{0,3},{1,2},{2,1},{3,0},{4,7},{5,6},{6,5},{7,4},{8,11},{9,10},{10,... | collective-permute-start | bytes 196616 | tf_op jit(solution)/shard_map/ppermute | solution.py:243
  21.3 23.5 %collective-permute-start.13 = (f32[128,128]{1,0:T(8,128)S(1)}, f32[128,128]{1,0:T(8,128)S(1)}, u32[]{:S(2)}, u32[]{:S(2)}) collective-permute-start(f32[128,128]{1,0:T(8,128)S(1)} %get-tuple-element.37), channel_id=1, source_target_pairs={{0,2},{1,3},{2,0},{3,1},{4,6},{5,7},{6,4},{7,5},{8,10},{9,11},{10,... | collective-permute-start | bytes 196616 | tf_op jit(solution)/shard_map/ppermute | solution.py:243
  21.8 23.8 %collective-permute-start.14 = (f32[128,128]{1,0:T(8,128)}, f32[128,128]{1,0:T(8,128)S(1)}, u32[]{:S(2)}, u32[]{:S(2)}) collective-permute-start(f32[128,128]{1,0:T(8,128)} %get-tuple-element.38), channel_id=1, source_target_pairs={{0,1},{1,0},{2,3},{3,2},{4,5},{5,4},{6,7},{7,6},{8,9},{9,8},{10,11... | collective-permute-start | bytes 196616 | tf_op jit(solution)/shard_map/ppermute | solution.py:243
  22.0 1.0 %copy-start.4 = (f32[8,16384]{1,0:T(8,128)S(1)}, f32[8,16384]{1,0:T(8,128)}, u32[]{:S(2)}) copy-start(f32[8,16384]{1,0:T(8,128)} %param.11) | copy-start | bytes 1572868
  23.0 0.7 copy-start.8
  23.7 2.2 %copy-start.9 = (f32[64,16384]{1,0:T(8,128)S(1)}, f32[64,16384]{1,0:T(8,128)}, u32[]{:S(2)}) copy-start(f32[64,16384]{1,0:T(8,128)} %param.12) | copy-start | bytes 12582916
  25.9 1.2 %copy-start.10 = (f32[16,16384]{1,0:T(8,128)S(1)}, f32[16,16384]{1,0:T(8,128)}, u32[]{:S(2)}) copy-start(f32[16,16384]{1,0:T(8,128)} %param.13) | copy-start | bytes 3145732
  27.1 0.7 copy-start.11
  27.7 0.7 copy-start.12
  28.4 0.7 copy-start.13
  35.6 2.0 %copy-start = (bf16[64,128,256]{2,1,0:T(8,128)(2,1)}, bf16[64,128,256]{2,1,0:T(8,128)(2,1)S(1)}, u32[]{:S(2)}) copy-start(bf16[64,128,256]{2,1,0:T(8,128)(2,1)S(1)} %get-tuple-element.26.refs_7_.refs_8_) | copy-start | bytes 12582916
  37.6 46.3 %collective-permute-start = (f32[128,128]{1,0:T(8,128)}, f32[128,128]{1,0:T(8,128)S(1)}, u32[]{:S(2)}, u32[]{:S(2)}) collective-permute-start(f32[128,128]{1,0:T(8,128)} %get-tuple-element.22), channel_id=1, source_target_pairs={{0,15},{1,14},{2,13},{3,12},{4,11},{5,10},{6,9},{7,8},{8,7},{9,6},... | collective-permute-start | bytes 196616 | tf_op jit(solution)/shard_map/ppermute | solution.py:243
  41.3 42.6 %collective-permute-start.1 = (f32[128,128]{1,0:T(8,128)}, f32[128,128]{1,0:T(8,128)S(1)}, u32[]{:S(2)}, u32[]{:S(2)}) collective-permute-start(f32[128,128]{1,0:T(8,128)} %get-tuple-element.23), channel_id=1, source_target_pairs={{0,14},{1,15},{2,12},{3,13},{4,10},{5,11},{6,8},{7,9},{8,6},{9,7},... | collective-permute-start | bytes 196616 | tf_op jit(solution)/shard_map/ppermute | solution.py:243
  42.2 41.7 %collective-permute-start.2 = (f32[128,128]{1,0:T(8,128)}, f32[128,128]{1,0:T(8,128)S(1)}, u32[]{:S(2)}, u32[]{:S(2)}) collective-permute-start(f32[128,128]{1,0:T(8,128)} %get-tuple-element.24), channel_id=1, source_target_pairs={{0,13},{1,12},{2,15},{3,14},{4,9},{5,8},{6,11},{7,10},{8,5},{9,4},... | collective-permute-start | bytes 196616 | tf_op jit(solution)/shard_map/ppermute | solution.py:243
  44.8 39.1 %collective-permute-start.3 = (f32[128,128]{1,0:T(8,128)}, f32[128,128]{1,0:T(8,128)S(1)}, u32[]{:S(2)}, u32[]{:S(2)}) collective-permute-start(f32[128,128]{1,0:T(8,128)} %get-tuple-element.25), channel_id=1, source_target_pairs={{0,12},{1,13},{2,14},{3,15},{4,8},{5,9},{6,10},{7,11},{8,4},{9,5},... | collective-permute-start | bytes 196616 | tf_op jit(solution)/shard_map/ppermute | solution.py:243
  45.6 33.8 %collective-permute-start.7 = (f32[128,128]{1,0:T(8,128)}, f32[128,128]{1,0:T(8,128)}, u32[]{:S(2)}, u32[]{:S(2)}) collective-permute-start(f32[128,128]{1,0:T(8,128)} %get-tuple-element.31), channel_id=1, source_target_pairs={{0,8},{1,9},{2,10},{3,11},{4,12},{5,13},{6,14},{7,15},{8,0},{9,1},... | collective-permute-start | bytes 196616 | tf_op jit(solution)/shard_map/ppermute | solution.py:243
  69.7 2.2 %copy-start.1 = (bf16[64,128,256]{2,1,0:T(8,128)(2,1)S(1)}, bf16[64,128,256]{2,1,0:T(8,128)(2,1)}, u32[]{:S(2)}) copy-start(bf16[64,128,256]{2,1,0:T(8,128)(2,1)} %copy-done) | copy-start | bytes 12582916
  71.9 3.3 %copy-start.2 = (bf16[64,128,256]{2,1,0:T(8,128)(2,1)S(1)}, bf16[64,128,256]{2,1,0:T(8,128)(2,1)}, u32[]{:S(2)}) copy-start(bf16[64,128,256]{2,1,0:T(8,128)(2,1)} %copy-done) | copy-start | bytes 12582916
  79.3 4.6 %copy-start.5 = (f32[8,16384]{1,0:T(8,128)S(1)}, f32[8,16384]{1,0:T(8,128)}, u32[]{:S(2)}) copy-start(f32[8,16384]{1,0:T(8,128)} %param.11) | copy-start | bytes 1572868
  89.1 3.1 %collective-permute-start.17 = (f32[8,128]{1,0:T(8,128)S(1)}, f32[8,128]{1,0:T(8,128)S(1)}, u32[]{:S(2)}, u32[]{:S(2)}) collective-permute-start(f32[8,128]{1,0:T(8,128)S(1)} %get-tuple-element.41), channel_id=1, source_target_pairs={{0,3},{1,2},{2,1},{3,0},{4,7},{5,6},{6,5},{7,4},{8,11},{9,10},{10,... | collective-permute-start | bytes 12296 | tf_op jit(solution)/shard_map/ppermute | solution.py:199
  89.1 3.7 %collective-permute-start.16 = (f32[8,128]{1,0:T(8,128)S(1)}, f32[8,128]{1,0:T(8,128)S(1)}, u32[]{:S(2)}, u32[]{:S(2)}) collective-permute-start(f32[8,128]{1,0:T(8,128)S(1)} %get-tuple-element.41), channel_id=1, source_target_pairs={{0,2},{1,3},{2,0},{3,1},{4,6},{5,7},{6,4},{7,5},{8,10},{9,11},{10,... | collective-permute-start | bytes 12296 | tf_op jit(solution)/shard_map/ppermute | solution.py:199
  91.0 1.8 %collective-permute-start.15 = (f32[8,128]{1,0:T(8,128)S(1)}, f32[8,128]{1,0:T(8,128)S(1)}, u32[]{:S(2)}, u32[]{:S(2)}) collective-permute-start(f32[8,128]{1,0:T(8,128)S(1)} %get-tuple-element.41), channel_id=1, source_target_pairs={{0,1},{1,0},{2,3},{3,2},{4,5},{5,4},{6,7},{7,6},{8,9},{9,8},{10,11... | collective-permute-start | bytes 12296 | tf_op jit(solution)/shard_map/ppermute | solution.py:199
  92.8 5.5 %collective-permute-start.20 = (f32[8,128]{1,0:T(8,128)S(1)}, f32[8,128]{1,0:T(8,128)S(1)}, u32[]{:S(2)}, u32[]{:S(2)}) collective-permute-start(f32[8,128]{1,0:T(8,128)S(1)} %add_add_fusion.refs_0_), channel_id=1, source_target_pairs={{0,12},{1,13},{2,14},{3,15},{4,8},{5,9},{6,10},{7,11},{8,4},{9,5},... | collective-permute-start | bytes 12296 | tf_op jit(solution)/shard_map/ppermute | solution.py:199
  92.9 5.4 %collective-permute-start.19 = (f32[8,128]{1,0:T(8,128)S(1)}, f32[8,128]{1,0:T(8,128)S(1)}, u32[]{:S(2)}, u32[]{:S(2)}) collective-permute-start(f32[8,128]{1,0:T(8,128)S(1)} %add_add_fusion.refs_0_), channel_id=1, source_target_pairs={{0,8},{1,9},{2,10},{3,11},{4,12},{5,13},{6,14},{7,15},{8,0},{9,1},... | collective-permute-start | bytes 12296 | tf_op jit(solution)/shard_map/ppermute | solution.py:199
  93.4 5.5 %collective-permute-start.18 = (f32[8,128]{1,0:T(8,128)S(1)}, f32[8,128]{1,0:T(8,128)S(1)}, u32[]{:S(2)}, u32[]{:S(2)}) collective-permute-start(f32[8,128]{1,0:T(8,128)S(1)} %add_add_fusion.refs_0_), channel_id=1, source_target_pairs={{0,4},{1,5},{2,6},{3,7},{4,0},{5,1},{6,2},{7,3},{8,12},{9,13},{10,... | collective-permute-start | bytes 12296 | tf_op jit(solution)/shard_map/ppermute | solution.py:199
  98.9 1.0 %copy-start.6 = (f32[1024,128]{1,0:T(8,128)S(1)}, f32[1024,128]{1,0:T(8,128)}, u32[]{:S(2)}) copy-start(f32[1024,128]{1,0:T(8,128)} %get-tuple-element.40.refs_4_) | copy-start | bytes 1572868

commit v3 on v1

v3 whole, which is shorter than its diff:
```python
import math

import jax
import jax.numpy as jnp
from jax import lax
from jax.experimental import pallas as pl
from jax.experimental.pallas import tpu as pltpu
from jax.sharding import PartitionSpec as P

F32 = jnp.float32
BF16 = jnp.bfloat16
SUB = 8
VMEM = pl.BlockSpec(memory_space=pltpu.VMEM)
SMEM = pl.BlockSpec(memory_space=pltpu.SMEM)
HBM = pl.BlockSpec(memory_space=pltpu.HBM)
MIB = 2**20


def as_rows(blocks, sector):
    count = blocks.shape[0]
    split = blocks.reshape(count // SUB, SUB, sector, sector)
    return split.transpose(0, 2, 1, 3).reshape(count * sector, sector)


def from_rows(rows, count):
    sector = rows.shape[1]
    split = rows.reshape(count // SUB, sector, SUB, sector)
    return split.transpose(0, 2, 1, 3).reshape(count, sector * sector)


def pick(ref, block):
    sector = ref.shape[1]
    start = (block // SUB) * (SUB * sector) + block % SUB
    return ref[pl.ds(start, sector, stride=SUB), :]


def halves(mat):
    high = mat.astype(BF16)
    low = (mat - high.astype(F32)).astype(BF16)
    return jnp.concatenate([high, low], axis=1)


def doubled(mat):
    both = halves(mat)
    return jnp.concatenate([both, both], axis=0)


def product(left, right):
    sector = right.shape[1] // 2
    wide = jnp.dot(left, right, preferred_element_type=F32)
    return wide[:, :sector] + wide[:, sector:]


def stacked(mat):
    high = mat.astype(BF16)
    low = (mat - high.astype(F32)).astype(BF16)
    rows = [jnp.concatenate([part, part], axis=1) for part in (high, low)]
    return jnp.concatenate(rows, axis=0)


def product_t(left, right):
    sector = right.shape[0] // 2
    wide = lax.dot_general(left, right, (((1,), (1,)), ((), ())), preferred_element_type=F32)
    return wide[:, :sector] + wide[:, sector:]


def roomy(mib):
    return pltpu.CompilerParams(vmem_limit_bytes=mib * MIB)


def gather_kernel(block_ref, psi_rows, out_hbm, stage, sems):
    puts = []
    for i in range(stage.shape[0]):
        stage[i] = pick(psi_rows, block_ref[i])
        put = pltpu.make_async_copy(stage.at[i], out_hbm.at[i], sems.at[i])
        put.start()
        puts.append(put)
    for put in puts:
        put.wait()


def local_kernel(block_ref, left_ref, right_ref, psi_rows, left_rows, right_rows, near_ref, sums_ref, rights_ref, psis_ref):
    def split_right(i, carry):
        rights_ref[i] = doubled(pick(right_rows, i))
        return carry

    lax.fori_loop(0, rights_ref.shape[0], split_right, 0, unroll=4)

    def split_psi(i, carry):
        psis_ref[i] = doubled(pick(psi_rows, i))
        return carry

    lax.fori_loop(0, psis_ref.shape[0], split_psi, 0, unroll=4)
    near_ref[...] = jnp.zeros_like(near_ref)

    def term(k, carry):
        block = block_ref[k]
        moved = product(halves(pick(left_rows, left_ref[k])), psis_ref[block])
        near_ref[block] += product(halves(moved), rights_ref[right_ref[k]])
        return carry

    lax.fori_loop(0, block_ref.shape[0], term, 0, unroll=4)
    corr = jnp.zeros((1, sums_ref.shape[1]), F32)
    norm = jnp.zeros((1, sums_ref.shape[1]), F32)
    for b in range(near_ref.shape[0]):
        mat = pick(psi_rows, b)
        corr += jnp.sum(mat * near_ref[b], axis=0, keepdims=True)
        norm += jnp.sum(mat * mat, axis=0, keepdims=True)
    row = lax.broadcasted_iota(jnp.int32, sums_ref.shape, 0)
    sums_ref[...] = jnp.where(row == 0, corr, jnp.where(row == 1, norm, 0.0))


def adjoint_kernel(terms, meta_ref, rindex_ref, out_index_ref, psi_rows, left_rows, right_rows, adjoint_ref, lefts_ref, rights_ref, psis_ref):
    sector = psi_rows.shape[1]

    def split_right(i, carry):
        rights_ref[i] = halves(pick(right_rows, i))
        return carry

    lax.fori_loop(0, rights_ref.shape[0], split_right, 0, unroll=4)

    def split_psi(i, carry):
        psis_ref[i] = stacked(pick(psi_rows, i))
        return carry

    lax.fori_loop(0, psis_ref.shape[0], split_psi, 0, unroll=4)

    def sender(i, carry):
        base = i * 2 * terms
        inner, weights = [], []
        for g in range(terms):
            left = halves(pick(left_rows, meta_ref[base + g]))
            lefts_ref[i, g * sector : (g + 1) * sector] = left
            weights += [left, left]
            live = meta_ref[base + terms + g].astype(F32)
            one = product_t(rights_ref[rindex_ref[i * terms + g]], psis_ref[out_index_ref[i * terms + g]])
            inner.append(halves(one * live))
        turned = product(jnp.concatenate(inner, axis=1), jnp.concatenate(weights, axis=0))
        adjoint_ref[i] = turned.T
        return carry

    lax.fori_loop(0, adjoint_ref.shape[0], sender, 0, unroll=2)


def overlap_kernel(came_ref, adjoint_ref, near_sums_ref, out_ref):
    def block(i, total):
        return total + jnp.sum((came_ref[i] * adjoint_ref[i]).reshape(-1, SUB, came_ref.shape[2]), axis=0)

    total = lax.fori_loop(0, came_ref.shape[0], block, jnp.zeros(out_ref.shape[1:], F32), unroll=4)
    corr = jnp.sum(total, axis=0, keepdims=True)
    row = lax.broadcasted_iota(jnp.int32, total.shape, 0)
    mine = near_sums_ref[...] + jnp.where(row == 0, corr, 0.0)
    for i in range(out_ref.shape[0]):
        out_ref[i] = mine


def remote_kernel(terms, meta_ref, rindex_ref, out_index_ref, came_ref, near_ref, lefts_ref, rights_ref, hpsi_rows, hpsi_hbm, acc, moved_ref, sem):
    count, sector, _ = came_ref.shape
    acc[...] = near_ref[...]

    def left_step(i, carry):
        moved = product(lefts_ref[i], doubled(came_ref[i]))
        for g in range(terms):
            live = meta_ref[i * 2 * terms + terms + g].astype(F32)
            moved_ref[i * terms + g] = halves(moved[g * sector : (g + 1) * sector] * live)
        return carry

    lax.fori_loop(0, count, left_step, 0, unroll=4)

    def right_step(t, carry):
        right = rights_ref[rindex_ref[t]]
        acc[out_index_ref[t]] += product(moved_ref[t], jnp.concatenate([right, right], axis=0))
        return carry

    lax.fori_loop(0, count * terms, right_step, 0, unroll=4)
    for b in range(acc.shape[0]):
        start = (b // SUB) * (SUB * sector) + b % SUB
        hpsi_rows[pl.ds(start, sector, stride=SUB), :] = acc[b]
    put = pltpu.make_async_copy(hpsi_rows, hpsi_hbm, sem)
    put.start()
    put.wait()


def residual_kernel(sums_ref, hpsi_rows, psi_rows, out_ref):
    total = jnp.sum(sums_ref[...], axis=0)
    whole = jnp.sum(total, axis=1, keepdims=True)
    theta = whole[0:1] / (whole[1:2] + 1e-06)
    out_ref[...] = hpsi_rows[...] - theta * psi_rows[...]


def shards(
    psi,
    left_env,
    right_env,
    send_block,
    send_left,
    send_live,
    recv_right,
    recv_out,
    loc_block,
    loc_left,
    loc_right,
):
    peers = lax.axis_size("renv")
    owned = psi.shape[0]
    sector = math.isqrt(psi.shape[1])
    slots = send_block.shape[1]
    terms = send_left.shape[2]
    count = peers * slots
    rights = right_env.shape[0]
    psi_rows = as_rows(psi, sector)
    left_rows = as_rows(left_env, sector)
    right_rows = as_rows(right_env, sector)
    rindex = recv_right.reshape(-1)
    out_index = recv_out.reshape(-1)
    blocks = jax.ShapeDtypeStruct((count, sector, sector), F32)
    rows = jax.ShapeDtypeStruct((owned * sector, sector), F32)
    mats = jax.ShapeDtypeStruct((owned, sector, sector), F32)
    tile = jax.ShapeDtypeStruct((SUB, sector), F32)

    sent = pl.pallas_call(
        gather_kernel,
        out_shape=blocks,
        in_specs=[SMEM, VMEM],
        out_specs=HBM,
        scratch_shapes=[pltpu.VMEM(blocks.shape, F32), pltpu.SemaphoreType.DMA((count,))],
        compiler_params=roomy(56),
        name="gather_blocks",
    )(send_block.reshape(-1), psi_rows)
    meta = jnp.concatenate([send_left, send_live], axis=2)
    sent, meta = lax.optimization_barrier((sent, meta))
    came = lax.all_to_all(sent.reshape(peers, slots, sector, sector), "renv", split_axis=0, concat_axis=0, tiled=True)
    came = came.reshape(count, sector, sector)
    meta = lax.all_to_all(meta, "renv", split_axis=0, concat_axis=0, tiled=True).reshape(-1)

    near, near_sums = pl.pallas_call(
        local_kernel,
        out_shape=(mats, tile),
        in_specs=[SMEM] * 3 + [VMEM] * 3,
        out_specs=(VMEM,) * 2,
        scratch_shapes=[
            pltpu.VMEM((rights, 2 * sector, 2 * sector), BF16),
            pltpu.VMEM((owned, 2 * sector, 2 * sector), BF16),
        ],
        compiler_params=roomy(56),
        cost_estimate=pl.CostEstimate(flops=4 * 10**9, bytes_accessed=6 * MIB, transcendentals=0),
        name="local_terms",
    )(loc_block, loc_left, loc_right, psi_rows, left_rows, right_rows)

    adjoint, left_parts, right_parts = pl.pallas_call(
        lambda *refs: adjoint_kernel(terms, *refs),
        out_shape=(
            blocks,
            jax.ShapeDtypeStruct((count, terms * sector, 2 * sector), BF16),
            jax.ShapeDtypeStruct((rights, sector, 2 * sector), BF16),
        ),
        in_specs=[SMEM] * 3 + [VMEM] * 3,
        out_specs=(VMEM,) * 3,
        scratch_shapes=[pltpu.VMEM((owned, 2 * sector, 2 * sector), BF16)],
        compiler_params=roomy(56),
        cost_estimate=pl.CostEstimate(flops=4 * 10**9, bytes_accessed=10 * MIB, transcendentals=0),
        name="adjoint_blocks",
    )(meta, rindex, out_index, psi_rows, left_rows, right_rows)

    sums = pl.pallas_call(
        overlap_kernel,
        out_shape=jax.ShapeDtypeStruct((peers, SUB, sector), F32),
        in_specs=[VMEM] * 3,
        out_specs=VMEM,
        compiler_params=roomy(24),
        name="overlap",
    )(came, adjoint, near_sums)
    sums = lax.all_to_all(sums, "renv", split_axis=0, concat_axis=0, tiled=True)

    hpsi_rows, hpsi = pl.pallas_call(
        lambda *refs: remote_kernel(terms, *refs),
        out_shape=(rows, rows),
        in_specs=[SMEM] * 3 + [VMEM] * 4,
        out_specs=(VMEM, HBM),
        scratch_shapes=[
            pltpu.VMEM(mats.shape, F32),
            pltpu.VMEM((count * terms, sector, 2 * sector), BF16),
            pltpu.SemaphoreType.DMA,
        ],
        compiler_params=roomy(56),
        cost_estimate=pl.CostEstimate(flops=4 * 10**9, bytes_accessed=6 * MIB, transcendentals=0),
        name="remote_terms",
    )(meta, rindex, out_index, came, near, left_parts, right_parts)

    residual_rows = pl.pallas_call(
        residual_kernel,
        out_shape=rows,
        in_specs=[VMEM] * 3,
        out_specs=VMEM,
        compiler_params=roomy(16),
        name="residual",
    )(sums, hpsi_rows, psi_rows)
    return (from_rows(hpsi, owned), from_rows(residual_rows, owned))


def solution(mesh):
    placed = (
        P(("groups", "renv"), None),
        P("groups", None),
        P(("groups", "renv"), None),
        P(("groups", "renv"), None),
        P(("groups", "renv"), None, None),
        P(("groups", "renv"), None, None),
        P(("groups", "renv"), None, None),
        P(("groups", "renv"), None, None),
        P(("groups", "renv")),
        P(("groups", "renv")),
        P(("groups", "renv")),
    )
    return jax.shard_map(
        shards,
        mesh=mesh,
        in_specs=placed,
        out_specs=(P(("groups", "renv"), None), P(("groups", "renv"), None)),
        check_vma=False,
    )
```

time: 67.2 us -> 62.8 us (0.935)
  Pallas kernels: 13.4 us -> 28.8 us
  local copies, waits for them, and re-layouts: 19.2 us -> 6.69 us
  waiting for transfers between devices: 7.25 us -> 0.85 us
    pallas_call x4 -> x6, Pallas kernels: 13.4 us -> 28.8 us  [the longest x1 10.2 us: shards(): pl.pallas_call(lambda *refs: adjoint_kernel(terms, *refs), out_shape=(blo...]
    unnamed x30 -> x12, local copies, waits for them, and re-layouts: 17.8 us -> 4.16 us
    all_to_all x1, waiting for transfers between devices: 4.47 us -> 0.85 us  [shards(): lax.all_to_all(sent.reshape(peers, slots, sector, sector), 'renv', split_...]
    all_to_all x1, waiting for transfers between devices: 2.78 us -> 0.01 us  [shards(): sums = lax.all_to_all(sums, 'renv', split_axis=0, concat_axis=0, tiled=True)]
    reshape x2, local copies, waits for them, and re-layouts: 0.17 us -> 1.27 us  [the longest x1 0.67 us: shards(): out_index = recv_out.reshape(-1)]
    concatenate x1 -> x0, local copies, waits for them, and re-layouts: 0.68 us -> none  [shards(): meta = jnp.concatenate([send_left, send_live], axis=2)]
  transfers between devices with their start and end apart: 2 -> 2, of which waited for: 2 -> 1; matrix products, arithmetic and copies ran while one was open for 4% -> 7% of each run, Pallas kernels for 11% -> 40%
where the time goes in v3:
time: 62.8 us; the launch traced here: 62.4 us
  Pallas kernels  28.8 us (46%)
  blocking collectives  13.6 us (22%)
  starting transfers between devices  10.5 us (17%)
  local copies, waits for them, and re-layouts  6.69 us (11%)
  other arithmetic  1.29 us (2%)
  waiting for transfers between devices  0.85 us (1%)
  between operations  0.72 us (1%)
    all_to_all x1, blocking collectives, shards(): lax.all_to_all(meta, 'renv', split_axis=0, concat_axis=0, tiled=True)  13.6 us
    pallas_call x1, Pallas kernels, shards(): pl.pallas_call(lambda *refs: adjoint_kernel(terms, *refs), out_shape=(blo...  10.2 us
    pallas_call x1, Pallas kernels, shards(): pl.pallas_call(lambda *refs: remote_kernel(terms, *refs), out_shape=(rows...  7.35 us
    pallas_call x1, Pallas kernels, shards(): pl.pallas_call(local_kernel, out_shape=(mats, tile), in_specs=[SMEM] * 3...  7.32 us
    all_to_all x1, starting transfers between devices, shards(): sums = lax.all_to_all(sums, 'renv', split_axis=0, concat_axis=0, tiled=True)  6.81 us
    unnamed x12, local copies, waits for them, and re-layouts  4.16 us
    all_to_all x1, starting transfers between devices, shards(): lax.all_to_all(sent.reshape(peers, slots, sector, sector), 'renv', split_...  3.65 us
    pallas_call x1, Pallas kernels, shards(): pl.pallas_call(gather_kernel, out_shape=blocks, in_specs=[SMEM, VMEM], ou...  2.21 us
  transfers between devices with their start and end apart: 2, of which 1 were waited for; matrix products, arithmetic and copies ran while one was open for 7% of the time, Pallas kernels for 40%

profile of v3, /device:TPU:0, one launch (start us, length us, event | category | flops | bytes accessed | tf_op | source)
XLA Modules:
  0.0 62.4 jit_solution(12997338264832672145)
XLA Ops:
  0.6 0.7 %pad_add_fusion = s32[16,1,4]{0,2,1:T(4,128)S(1)} fusion(s32[16,1,2]{0,2,1:T(2,128)} %param.16, s32[16,1,2]{0,2,1:T(2,128)} %param.15), kind=kLoop, calls=%fused_computation | loop fusion | flops 64 | bytes 512 | tf_op jit(solution)/shard_map/concatenate | solution.py:230
  1.3 2.2 %gather_blocks.1 = f32[16,128,128]{2,1,0:T(8,128)} custom-call(s32[16]{0:T(128)} %bitcast.42, f32[1024,128]{1,0:T(8,128)} %bitcast.36), custom_call_target="tpu_custom_call" | custom-call | tf_op jit(solution)/shard_map/gather_blocks/pallas_call | solution.py:221
  3.6 0.1 copy.24
  3.6 13.6 %all_to_all.15 = s32[16,1,4]{2,1,0:T(1,128)S(1)} all-to-all(s32[16,1,4]{2,1,0:T(1,128)S(1)} %copy.24), channel_id=1, replica_groups=mesh['groups'=2,'renv'=16] {'renv'}, dimensions={0} | all-to-all | bytes 512 | tf_op jit(solution)/shard_map/all_to_all | solution.py:234
  17.2 3.7 %all-to-all-start.1 = ((f32[16,1,128,128]{3,2,1,0:T(8,128)}), f32[16,1,128,128]{3,2,1,0:T(8,128)S(1)}, u32[]{:S(2)}, u32[]{:S(2)}) async-start(f32[16,1,128,128]{3,2,1,0:T(8,128)} %bitcast.40), calls=%async_computation.1 | async-start | bytes 2097152 | tf_op jit(solution)/shard_map/all_to_all | solution.py:232
  20.9 0.8 %copy.25 = s32[16,1,2]{2,0,1:T(8,128)S(1)} copy(s32[16,1,2]{0,2,1:T(2,128)} %param.17) | data formatting | bytes 256 | tf_op args[6]
  21.6 0.6 reshape.56.refs_1_
  22.2 0.8 %copy.26 = s32[16,1,2]{2,0,1:T(8,128)S(1)} copy(s32[16,1,2]{0,2,1:T(2,128)} %param.18) | data formatting | bytes 256 | tf_op args[7]
  23.0 0.7 %reshape.57.refs_2_ = s32[32]{0:T(128)} reshape(s32[16,1,2]{2,0,1:T(8,128)S(1)} %copy.26) | data formatting | bytes 256 | tf_op jit(solution)/shard_map/reshape | solution.py:215
  23.6 7.3 %local_terms.1 = (f32[8,128,128]{2,1,0:T(8,128)}, f32[8,128]{1,0:T(8,128)}) custom-call(s32[32]{0:T(128)} %block_ref.1, s32[32]{0:T(128)} %left_ref.1, s32[32]{0:T(128)} %right_ref.1, f32[1024,128]{1,0:T(8,128)} %bitcast.37, f32[8192,128]{1,0:T(8,128)} %bitcast.43, f32[2048,128]{1,0:T(8,128)} %bitcast.45), custom_call_target="tpu_custom_call" | custom-call | flops 4000000000 | bytes 6291456 | tf_op jit(solution)/shard_map/local_terms/pallas_call | solution.py:236
  31.0 0.5 broadcast.3
  31.5 0.6 reduce.3
  32.1 0.7 %reshape.55.refs_0_ = s32[64]{0:T(128)} reshape(s32[16,4]{1,0:T(8,128)S(1)} %reduce.3) | data formatting | bytes 512 | tf_op jit(solution)/shard_map/reshape | solution.py:234
  32.7 0.0 copy-start.4
  32.7 10.2 %adjoint_blocks.1 = (f32[16,128,128]{2,1,0:T(8,128)}, bf16[16,256,256]{2,1,0:T(8,128)(2,1)}, bf16[16,128,256]{2,1,0:T(8,128)(2,1)}) custom-call(s32[64]{0:T(128)} %reshape.55.refs_0_, s32[32]{0:T(128)} %reshape.56.refs_1_, s32[32]{0:T(128)} %reshape.57.refs_2_, f32[1024,128]{1,0:T(8,128)} %bitcast.38, f32[8192,128]{1,0:T(8,128)} %bitcast.44, ...), custom_call_target="tpu_custom_call" | custom-call | flops 4000000000 | bytes 10485760 | tf_op jit(solution)/shard_map/adjoint_blocks/pallas_call | solution.py:250
  42.9 0.9 %all-to-all-done.1 = f32[16,1,128,128]{3,2,1,0:T(8,128)S(1)} async-done(((f32[16,1,128,128]{3,2,1,0:T(8,128)}), f32[16,1,128,128]{3,2,1,0:T(8,128)S(1)}, u32[]{:S(2)}, u32[]{:S(2)}) %all-to-all-start.1) | async-done | bytes 1048608 | tf_op jit(solution)/shard_map/all_to_all | solution.py:232
  43.8 0.0 copy-start
  43.8 0.0 copy-done.4
  43.8 0.0 copy-start.2
  43.8 1.6 %copy-done.2 = f32[16,128,128]{2,1,0:T(8,128)S(1)} copy-done((f32[16,128,128]{2,1,0:T(8,128)S(1)}, f32[16,128,128]{2,1,0:T(8,128)}, u32[]{:S(2)}) %copy-start.2) | copy-done | bytes 1048600
  45.4 0.8 %overlap.1 = f32[16,8,128]{2,1,0:T(8,128)} custom-call(f32[16,128,128]{2,1,0:T(8,128)S(1)} %bitcast.34, f32[16,128,128]{2,1,0:T(8,128)S(1)} %copy-done.2, f32[8,128]{1,0:T(8,128)S(1)} %copy-done.4), custom_call_target="tpu_custom_call" | custom-call | tf_op jit(solution)/shard_map/overlap/pallas_call | solution.py:265
  46.1 6.8 %all-to-all-start.2 = ((f32[16,8,128]{2,1,0:T(8,128)}), f32[16,8,128]{2,1,0:T(8,128)S(1)}, u32[]{:S(2)}, u32[]{:S(2)}) async-start(f32[16,8,128]{2,1,0:T(8,128)} %overlap.1), calls=%async_computation.2 | async-start | bytes 131072 | tf_op jit(solution)/shard_map/all_to_all | solution.py:273
  52.9 0.0 copy-done
  52.9 0.0 copy-start.1
  53.0 7.3 %remote_terms.1 = (f32[1024,128]{1,0:T(8,128)}, f32[1024,128]{1,0:T(8,128)}) custom-call(s32[64]{0:T(128)} %reshape.55.refs_0_, s32[32]{0:T(128)} %reshape.56.refs_1_, s32[32]{0:T(128)} %reshape.57.refs_2_, f32[16,128,128]{2,1,0:T(8,128)} %bitcast.35, f32[8,128,128]{2,1,0:T(8,128)} %get-tuple-element.13.refs_4_, ...), custom_call_target="tpu_custom_call" | custom-call | flops 4000000000 | bytes 6291456 | tf_op jit(solution)/shard_map/remote_terms/pallas_call | solution.py:275
  60.3 0.0 all-to-all-done.2.sums_ref
  60.3 0.0 copy-done.1
  60.3 0.0 copy-start.3
  60.3 1.0 %copy-done.3 = f32[1024,128]{1,0:T(8,128)S(1)} copy-done((f32[1024,128]{1,0:T(8,128)S(1)}, f32[1024,128]{1,0:T(8,128)}, u32[]{:S(2)}) %copy-start.3) | copy-done | bytes 524312
  61.4 1.0 %residual.1 = f32[1024,128]{1,0:T(8,128)} custom-call(f32[16,8,128]{2,1,0:T(8,128)S(1)} %all-to-all-done.2.sums_ref, f32[1024,128]{1,0:T(8,128)S(1)} %copy-done.3, f32[1024,128]{1,0:T(8,128)S(1)} %bitcast.39), custom_call_target="tpu_custom_call" | custom-call | tf_op jit(solution)/shard_map/residual/pallas_call | solution.py:290
Async XLA Ops:
  17.2 26.6 %all-to-all-start.1 = ((f32[16,1,128,128]{3,2,1,0:T(8,128)}), f32[16,1,128,128]{3,2,1,0:T(8,128)S(1)}, u32[]{:S(2)}, u32[]{:S(2)}) async-start(f32[16,1,128,128]{3,2,1,0:T(8,128)} %bitcast.40), calls=%async_computation.1 | async-start | bytes 2097152 | tf_op jit(solution)/shard_map/all_to_all | solution.py:232
  32.7 11.0 %copy-start.4 = (f32[8,128]{1,0:T(8,128)S(1)}, f32[8,128]{1,0:T(8,128)}, u32[]{:S(2)}) copy-start(f32[8,128]{1,0:T(8,128)} %get-tuple-element.18.near_sums_ref) | copy-start | bytes 12292
  43.8 9.2 %copy-start = (f32[16,1,128,128]{3,2,1,0:T(8,128)}, f32[16,1,128,128]{3,2,1,0:T(8,128)S(1)}, u32[]{:S(2)}) copy-start(f32[16,1,128,128]{3,2,1,0:T(8,128)S(1)} %all-to-all-done.1) | copy-start | bytes 3145732
  43.8 1.6 %copy-start.2 = (f32[16,128,128]{2,1,0:T(8,128)S(1)}, f32[16,128,128]{2,1,0:T(8,128)}, u32[]{:S(2)}) copy-start(f32[16,128,128]{2,1,0:T(8,128)} %get-tuple-element.17.adjoint_ref) | copy-start | bytes 3145732
  46.1 14.2 %all-to-all-start.2 = ((f32[16,8,128]{2,1,0:T(8,128)}), f32[16,8,128]{2,1,0:T(8,128)S(1)}, u32[]{:S(2)}, u32[]{:S(2)}) async-start(f32[16,8,128]{2,1,0:T(8,128)} %overlap.1), calls=%async_computation.2 | async-start | bytes 131072 | tf_op jit(solution)/shard_map/all_to_all | solution.py:273
  52.9 7.4 %copy-start.1 = (f32[8,16384]{1,0:T(8,128)S(1)}, f32[8,16384]{1,0:T(8,128)}, u32[]{:S(2)}) copy-start(f32[8,16384]{1,0:T(8,128)} %param.11) | copy-start | bytes 1572868
  60.3 1.0 %copy-start.3 = (f32[1024,128]{1,0:T(8,128)S(1)}, f32[1024,128]{1,0:T(8,128)}, u32[]{:S(2)}) copy-start(f32[1024,128]{1,0:T(8,128)} %get-tuple-element.19.hpsi_rows) | copy-start | bytes 1572868

commit v4 on v3

--- a/solution.py
+++ b/solution.py
@@ -62,6 +62,10 @@
     sector = right.shape[0] // 2
     wide = lax.dot_general(left, right, (((1,), (1,)), ((), ())), preferred_element_type=F32)
     return wide[:, :sector] + wide[:, sector:]
+
+
+def twice(part):
+    return jnp.concatenate([part, part], axis=0)
 
 
 def roomy(mib):
@@ -79,27 +83,61 @@
         put.wait()
 
 
-def local_kernel(block_ref, left_ref, right_ref, psi_rows, left_rows, right_rows, near_ref, sums_ref, rights_ref, psis_ref):
+def turn_kernel(left_ref, live_ref, rindex_ref, out_index_ref, psi_rows, right_rows, meta_ref, turned_ref, rights_ref, psis_ref, stacks_ref):
+    slots, terms, _ = left_ref.shape
+    width = meta_ref.shape[2]
+    lane = lax.broadcasted_iota(jnp.int32, (1, width), 1)
+
+    def row(i, carry):
+        values = jnp.zeros((1, width), jnp.int32)
+        for g in range(terms):
+            values = jnp.where(lane == g, left_ref[i % slots, g, i // slots], values)
+            values = jnp.where(lane == terms + g, live_ref[i % slots, g, i // slots], values)
+        meta_ref[i] = values
+        return carry
+
+    lax.fori_loop(0, meta_ref.shape[0], row, 0, unroll=4)
+
     def split_right(i, carry):
-        rights_ref[i] = doubled(pick(right_rows, i))
+        rights_ref[i] = halves(pick(right_rows, i))
         return carry
 
     lax.fori_loop(0, rights_ref.shape[0], split_right, 0, unroll=4)
 
     def split_psi(i, carry):
-        psis_ref[i] = doubled(pick(psi_rows, i))
+        mat = pick(psi_rows, i)
+        psis_ref[i] = halves(mat)
+        stacks_ref[i] = stacked(mat)
         return carry
 
     lax.fori_loop(0, psis_ref.shape[0], split_psi, 0, unroll=4)
+
+    def turn(i, carry):
+        inner = []
+        for g in range(terms):
+            right = rights_ref[rindex_ref[i % slots, g, i // slots]]
+            inner.append(halves(product_t(right, stacks_ref[out_index_ref[i % slots, g, i // slots]])))
+        turned_ref[i] = jnp.concatenate(inner, axis=1)
+        return carry
+
+    lax.fori_loop(0, turned_ref.shape[0], turn, 0, unroll=4)
+
+
+def local_kernel(block_ref, left_ref, right_ref, psi_rows, left_rows, psis_ref, rights_ref, near_ref, sums_ref, moved_ref):
     near_ref[...] = jnp.zeros_like(near_ref)
 
-    def term(k, carry):
-        block = block_ref[k]
-        moved = product(halves(pick(left_rows, left_ref[k])), psis_ref[block])
-        near_ref[block] += product(halves(moved), rights_ref[right_ref[k]])
-        return carry
-
-    lax.fori_loop(0, block_ref.shape[0], term, 0, unroll=4)
+    def left_step(k, carry):
+        moved = product(halves(pick(left_rows, left_ref[k])), twice(psis_ref[block_ref[k]]))
+        moved_ref[k] = halves(moved)
+        return carry
+
+    lax.fori_loop(0, block_ref.shape[0], left_step, 0, unroll=8)
+
+    def right_step(k, carry):
+        near_ref[block_ref[k]] += product(moved_ref[k], twice(rights_ref[right_ref[k]]))
+        return carry
+
+    lax.fori_loop(0, block_ref.shape[0], right_step, 0, unroll=8)
     corr = jnp.zeros((1, sums_ref.shape[1]), F32)
     norm = jnp.zeros((1, sums_ref.shape[1]), F32)
     for b in range(near_ref.shape[0]):
@@ -110,36 +148,20 @@
     sums_ref[...] = jnp.where(row == 0, corr, jnp.where(row == 1, norm, 0.0))
 
 
-def adjoint_kernel(terms, meta_ref, rindex_ref, out_index_ref, psi_rows, left_rows, right_rows, adjoint_ref, lefts_ref, rights_ref, psis_ref):
-    sector = psi_rows.shape[1]
-
-    def split_right(i, carry):
-        rights_ref[i] = halves(pick(right_rows, i))
-        return carry
-
-    lax.fori_loop(0, rights_ref.shape[0], split_right, 0, unroll=4)
-
-    def split_psi(i, carry):
-        psis_ref[i] = stacked(pick(psi_rows, i))
-        return carry
-
-    lax.fori_loop(0, psis_ref.shape[0], split_psi, 0, unroll=4)
+def adjoint_kernel(terms, meta_ref, left_rows, turned_ref, adjoint_ref, lefts_ref):
+    sector = left_rows.shape[1]
 
     def sender(i, carry):
-        base = i * 2 * terms
-        inner, weights = [], []
+        weights = []
         for g in range(terms):
-            left = halves(pick(left_rows, meta_ref[base + g]))
+            live = meta_ref[i, 0, terms + g].astype(F32)
+            left = halves(pick(left_rows, meta_ref[i, 0, g]) * live)
             lefts_ref[i, g * sector : (g + 1) * sector] = left
-            weights += [left, left]
-            live = meta_ref[base + terms + g].astype(F32)
-            one = product_t(rights_ref[rindex_ref[i * terms + g]], psis_ref[out_index_ref[i * terms + g]])
-            inner.append(halves(one * live))
-        turned = product(jnp.concatenate(inner, axis=1), jnp.concatenate(weights, axis=0))
-        adjoint_ref[i] = turned.T
-        return carry
-
-    lax.fori_loop(0, adjoint_ref.shape[0], sender, 0, unroll=2)
+            weights.append(twice(left))
+        adjoint_ref[i] = product(turned_ref[i], jnp.concatenate(weights, axis=0)).T
+        return carry
+
+    lax.fori_loop(0, adjoint_ref.shape[0], sender, 0, unroll=4)
 
 
 def overlap_kernel(came_ref, adjoint_ref, near_sums_ref, out_ref):
@@ -154,25 +176,24 @@
         out_ref[i] = mine
 
 
-def remote_kernel(terms, meta_ref, rindex_ref, out_index_ref, came_ref, near_ref, lefts_ref, rights_ref, hpsi_rows, hpsi_hbm, acc, moved_ref, sem):
+def remote_kernel(rindex_ref, out_index_ref, came_ref, near_ref, lefts_ref, rights_ref, hpsi_rows, hpsi_hbm, acc, moved_ref, sem):
     count, sector, _ = came_ref.shape
+    slots, terms, _ = rindex_ref.shape
     acc[...] = near_ref[...]
 
     def left_step(i, carry):
-        moved = product(lefts_ref[i], doubled(came_ref[i]))
+        moved_ref[i] = halves(product(lefts_ref[i], doubled(came_ref[i])))
+        return carry
+
+    lax.fori_loop(0, count, left_step, 0, unroll=4)
+
+    def right_step(i, carry):
         for g in range(terms):
-            live = meta_ref[i * 2 * terms + terms + g].astype(F32)
-            moved_ref[i * terms + g] = halves(moved[g * sector : (g + 1) * sector] * live)
-        return carry
-
-    lax.fori_loop(0, count, left_step, 0, unroll=4)
-
-    def right_step(t, carry):
-        right = rights_ref[rindex_ref[t]]
-        acc[out_index_ref[t]] += product(moved_ref[t], jnp.concatenate([right, right], axis=0))
-        return carry
-
-    lax.fori_loop(0, count * terms, right_step, 0, unroll=4)
+            right = rights_ref[rindex_ref[i % slots, g, i // slots]]
+            acc[out_index_ref[i % slots, g, i // slots]] += product(moved_ref[i, g * sector : (g + 1) * sector], twice(right))
+        return carry
+
+    lax.fori_loop(0, count, right_step, 0, unroll=4)
     for b in range(acc.shape[0]):
         start = (b // SUB) * (SUB * sector) + b % SUB
         hpsi_rows[pl.ds(start, sector, stride=SUB), :] = acc[b]
@@ -211,8 +232,7 @@
     psi_rows = as_rows(psi, sector)
     left_rows = as_rows(left_env, sector)
     right_rows = as_rows(right_env, sector)
-    rindex = recv_right.reshape(-1)
-    out_index = recv_out.reshape(-1)
+    by_slot = [index.transpose(1, 2, 0) for index in (send_left, send_live, recv_right, recv_out)]
     blocks = jax.ShapeDtypeStruct((count, sector, sector), F32)
     rows = jax.ShapeDtypeStruct((owned * sector, sector), F32)
     mats = jax.ShapeDtypeStruct((owned, sector, sector), F32)
@@ -227,40 +247,46 @@
         compiler_params=roomy(56),
         name="gather_blocks",
     )(send_block.reshape(-1), psi_rows)
-    meta = jnp.concatenate([send_left, send_live], axis=2)
-    sent, meta = lax.optimization_barrier((sent, meta))
     came = lax.all_to_all(sent.reshape(peers, slots, sector, sector), "renv", split_axis=0, concat_axis=0, tiled=True)
     came = came.reshape(count, sector, sector)
-    meta = lax.all_to_all(meta, "renv", split_axis=0, concat_axis=0, tiled=True).reshape(-1)
+
+    meta, turned, right_parts, psi_parts = pl.pallas_call(
+        turn_kernel,
+        out_shape=(
+            jax.ShapeDtypeStruct((count, 1, sector), jnp.int32),
+            jax.ShapeDtypeStruct((count, sector, terms * 2 * sector), BF16),
+            jax.ShapeDtypeStruct((rights, sector, 2 * sector), BF16),
+            jax.ShapeDtypeStruct((owned, sector, 2 * sector), BF16),
+        ),
+        in_specs=[SMEM] * 4 + [VMEM] * 2,
+        out_specs=(VMEM,) * 4,
+        scratch_shapes=[pltpu.VMEM((owned, 2 * sector, 2 * sector), BF16)],
+        compiler_params=roomy(56),
+        cost_estimate=pl.CostEstimate(flops=4 * 10**9, bytes_accessed=6 * MIB, transcendentals=0),
+        name="turn",
+    )(*by_slot, psi_rows, right_rows)
+    meta = lax.all_to_all(meta, "renv", split_axis=0, concat_axis=0, tiled=True)
 
     near, near_sums = pl.pallas_call(
         local_kernel,
         out_shape=(mats, tile),
-        in_specs=[SMEM] * 3 + [VMEM] * 3,
+        in_specs=[SMEM] * 3 + [VMEM] * 4,
         out_specs=(VMEM,) * 2,
-        scratch_shapes=[
-            pltpu.VMEM((rights, 2 * sector, 2 * sector), BF16),
-            pltpu.VMEM((owned, 2 * sector, 2 * sector), BF16),
-        ],
+        scratch_shapes=[pltpu.VMEM((loc_block.shape[0], sector, 2 * sector), BF16)],
         compiler_params=roomy(56),
         cost_estimate=pl.CostEstimate(flops=4 * 10**9, bytes_accessed=6 * MIB, transcendentals=0),
         name="local_terms",
-    )(loc_block, loc_left, loc_right, psi_rows, left_rows, right_rows)
-
-    adjoint, left_parts, right_parts = pl.pallas_call(
+    )(loc_block, loc_left, loc_right, psi_rows, left_rows, psi_parts, right_parts)
+
+    adjoint, left_parts = pl.pallas_call(
         lambda *refs: adjoint_kernel(terms, *refs),
-        out_shape=(
-            blocks,
-            jax.ShapeDtypeStruct((count, terms * sector, 2 * sector), BF16),
-            jax.ShapeDtypeStruct((rights, sector, 2 * sector), BF16),
-        ),
-        in_specs=[SMEM] * 3 + [VMEM] * 3,
-        out_specs=(VMEM,) * 3,
-        scratch_shapes=[pltpu.VMEM((owned, 2 * sector, 2 * sector), BF16)],
-        compiler_params=roomy(56),
+        out_shape=(blocks, jax.ShapeDtypeStruct((count, terms * sector, 2 * sector), BF16)),
+        in_specs=[SMEM] + [VMEM] * 2,
+        out_specs=(VMEM,) * 2,
+        compiler_params=roomy(48),
         cost_estimate=pl.CostEstimate(flops=4 * 10**9, bytes_accessed=10 * MIB, transcendentals=0),
         name="adjoint_blocks",
-    )(meta, rindex, out_index, psi_rows, left_rows, right_rows)
+    )(meta, left_rows, turned)
 
     sums = pl.pallas_call(
         overlap_kernel,
@@ -273,19 +299,19 @@
     sums = lax.all_to_all(sums, "renv", split_axis=0, concat_axis=0, tiled=True)
 
     hpsi_rows, hpsi = pl.pallas_call(
-        lambda *refs: remote_kernel(terms, *refs),
+        remote_kernel,
         out_shape=(rows, rows),
-        in_specs=[SMEM] * 3 + [VMEM] * 4,
+        in_specs=[SMEM] * 2 + [VMEM] * 4,
         out_specs=(VMEM, HBM),
         scratch_shapes=[
             pltpu.VMEM(mats.shape, F32),
-            pltpu.VMEM((count * terms, sector, 2 * sector), BF16),
+            pltpu.VMEM((count, terms * sector, 2 * sector), BF16),
             pltpu.SemaphoreType.DMA,
         ],
-        compiler_params=roomy(56),
+        compiler_params=roomy(48),
         cost_estimate=pl.CostEstimate(flops=4 * 10**9, bytes_accessed=6 * MIB, transcendentals=0),
         name="remote_terms",
-    )(meta, rindex, out_index, came, near, left_parts, right_parts)
+    )(*by_slot[2:], came, near, left_parts, right_parts)
 
     residual_rows = pl.pallas_call(
         residual_kernel,

time: 62.8 us -> 62.5 us (level)
  waiting for transfers between devices: 0.85 us -> 15.5 us
  blocking collectives: 13.6 us -> 0 us
  starting transfers between devices: 10.5 us -> 17.8 us
  Pallas kernels: 28.8 us -> 24 us
  local copies, waits for them, and re-layouts: 6.69 us -> 3.98 us
  other arithmetic: 1.29 us -> 0 us
    all_to_all x1 -> x0, blocking collectives: 13.6 us -> none  [shards(): lax.all_to_all(meta, 'renv', split_axis=0, concat_axis=0, tiled=True)]
    all_to_all x1, waiting for transfers between devices: 0.85 us -> 11.2 us  [shards(): lax.all_to_all(sent.reshape(peers, slots, sector, sector), 'renv', split_...]
    all_to_all x0 -> x1, starting transfers between devices: none -> 7.36 us  [shards(): meta = lax.all_to_all(meta, 'renv', split_axis=0, concat_axis=0, tiled=True)]
    pallas_call x1, Pallas kernels: 10.2 us -> 3.92 us  [shards(): pl.pallas_call(lambda *refs: adjoint_kernel(terms, *refs), out_shape=(blo...]
    all_to_all x0 -> x1, waiting for transfers between devices: none -> 4.1 us  [shards(): meta = lax.all_to_all(meta, 'renv', split_axis=0, concat_axis=0, tiled=True)]
    pallas_call x1 -> x2, Pallas kernels: 7.35 us -> 9.63 us  [the longest x1 5.58 us: shards(): pl.pallas_call(turn_kernel, out_shape=(jax.ShapeDtypeStruct((count, 1, se...]
    reshape x3 -> x0, local copies, waits for them, and re-layouts: 1.94 us -> none  [the longest x1 0.67 us: shards(): out_index = recv_out.reshape(-1)]
    pallas_call x1, Pallas kernels: 7.32 us -> 6.38 us  [shards(): pl.pallas_call(local_kernel, out_shape=(mats, tile), in_specs=[SMEM] * 3...]
  transfers between devices with their start and end apart: 2 -> 3, of which waited for: 1 -> 3; matrix products, arithmetic and copies ran while one was open for 7% -> 0% of each run, Pallas kernels for 40% -> 27%
where the time goes in v4:
time: 62.5 us; the launch traced here: 62 us
  Pallas kernels  24 us (38%)
  starting transfers between devices  17.8 us (28%)
  waiting for transfers between devices  15.5 us (25%)
  local copies, waits for them, and re-layouts  3.98 us (6%)
  between operations  0.73 us (1%)
    all_to_all x1, waiting for transfers between devices, shards(): lax.all_to_all(sent.reshape(peers, slots, sector, sector), 'renv', split_...  11.2 us
    all_to_all x1, starting transfers between devices, shards(): meta = lax.all_to_all(meta, 'renv', split_axis=0, concat_axis=0, tiled=True)  7.36 us
    all_to_all x1, starting transfers between devices, shards(): sums = lax.all_to_all(sums, 'renv', split_axis=0, concat_axis=0, tiled=True)  6.81 us
    pallas_call x1, Pallas kernels, shards(): pl.pallas_call(local_kernel, out_shape=(mats, tile), in_specs=[SMEM] * 3...  6.38 us
    pallas_call x1, Pallas kernels, shards(): pl.pallas_call(turn_kernel, out_shape=(jax.ShapeDtypeStruct((count, 1, se...  5.58 us
    all_to_all x1, waiting for transfers between devices, shards(): meta = lax.all_to_all(meta, 'renv', split_axis=0, concat_axis=0, tiled=True)  4.1 us
    pallas_call x1, Pallas kernels, shards(): pl.pallas_call(remote_kernel, out_shape=(rows, rows), in_specs=[SMEM] * 2...  4.04 us
    unnamed x18, local copies, waits for them, and re-layouts  3.98 us
  transfers between devices with their start and end apart: 3, of which 3 were waited for; matrix products, arithmetic and copies ran while one was open for 0% of the time, Pallas kernels for 27%

profile of v4, /device:TPU:0, one launch (start us, length us, event | category | flops | bytes accessed | tf_op | source)
XLA Modules:
  0.0 62.0 jit_solution(11025504399442581899)
XLA Ops:
  0.6 5.6 %turn.1 = (s32[16,1,128]{2,1,0:T(1,128)}, bf16[16,128,512]{2,1,0:T(8,128)(2,1)}, bf16[16,128,256]{2,1,0:T(8,128)(2,1)}, bf16[8,128,256]{2,1,0:T(8,128)(2,1)}) custom-call(s32[1,2,16]{2,1,0:T(2,128)} %bitcast.50, s32[1,2,16]{2,1,0:T(2,128)} %bitcast.51, s32[1,2,16]{2,1,0:T(2,128)} %bitcast.40, s32[1,2,16]{2,1,0:T(2,128)} %bitcast.42, f32[1024,128]{1,0:T(8,128)} %bitcast.36, ...), custom_call_target="tpu_custom_call" | custom-call | flops 4000000000 | bytes 6291456 | tf_op jit(solution)/shard_map/turn/pallas_call | solution.py:253
  6.2 7.4 %all-to-all-start.1 = ((s32[16,1,128]{2,1,0:T(1,128)}), s32[16,1,128]{2,1,0:T(1,128)S(1)}, u32[]{:S(2)}, u32[]{:S(2)}) async-start(s32[16,1,128]{2,1,0:T(1,128)} %get-tuple-element.15), calls=%async_computation.1 | async-start | bytes 16384 | tf_op jit(solution)/shard_map/all_to_all | solution.py:268
  13.6 2.2 %gather_blocks.1 = f32[16,128,128]{2,1,0:T(8,128)} custom-call(s32[16]{0:T(128)} %bitcast.46, f32[1024,128]{1,0:T(8,128)} %bitcast.37), custom_call_target="tpu_custom_call" | custom-call | tf_op jit(solution)/shard_map/gather_blocks/pallas_call | solution.py:241
  15.8 4.1 %all-to-all-done.1.refs_0_ = s32[16,1,128]{2,1,0:T(1,128)S(1)} async-done(((s32[16,1,128]{2,1,0:T(1,128)}), s32[16,1,128]{2,1,0:T(1,128)S(1)}, u32[]{:S(2)}, u32[]{:S(2)}) %all-to-all-start.1) | async-done | bytes 8224 | tf_op jit(solution)/shard_map/all_to_all | solution.py:268
  19.9 3.7 %all-to-all-start = ((f32[16,1,128,128]{3,2,1,0:T(8,128)}), f32[16,1,128,128]{3,2,1,0:T(8,128)S(1)}, u32[]{:S(2)}, u32[]{:S(2)}) async-start(f32[16,1,128,128]{3,2,1,0:T(8,128)} %bitcast.44), calls=%async_computation | async-start | bytes 2097152 | tf_op jit(solution)/shard_map/all_to_all | solution.py:250
  23.6 0.0 copy-start.4
  23.6 6.4 %local_terms.1 = (f32[8,128,128]{2,1,0:T(8,128)}, f32[8,128]{1,0:T(8,128)}) custom-call(s32[32]{0:T(128)} %block_ref.1, s32[32]{0:T(128)} %left_ref.1, s32[32]{0:T(128)} %right_ref.1, f32[1024,128]{1,0:T(8,128)} %bitcast.38, f32[8192,128]{1,0:T(8,128)} %bitcast.47, bf16[8,128,256]{2,1,0:T(8,128)(2,1)} %get-tuple-element.12.psis_ref, ...), custom_call_target="tpu_custom_call" | custom-call | flops 4000000000 | bytes 6291456 | tf_op jit(solution)/shard_map/local_terms/pallas_call | solution.py:270
  30.0 0.0 copy-done.4
  30.0 0.0 copy-start.1
  30.0 3.9 %adjoint_blocks.1 = (f32[16,128,128]{2,1,0:T(8,128)S(1)}, bf16[16,256,256]{2,1,0:T(8,128)(2,1)S(1)}) custom-call(s32[16,1,128]{2,1,0:T(1,128)S(1)} %all-to-all-done.1.refs_0_, f32[8192,128]{1,0:T(8,128)} %bitcast.48, bf16[16,128,512]{2,1,0:T(8,128)(2,1)S(1)} %copy-done.4), custom_call_target="tpu_custom_call" | custom-call | flops 4000000000 | bytes 10485760 | tf_op jit(solution)/shard_map/adjoint_blocks/pallas_call | solution.py:281
  33.9 0.0 copy-start.5
  33.9 1.3 %copy-done.5 = bf16[16,256,256]{2,1,0:T(8,128)(2,1)} copy-done((bf16[16,256,256]{2,1,0:T(8,128)(2,1)}, bf16[16,256,256]{2,1,0:T(8,128)(2,1)S(1)}, u32[]{:S(2)}) %copy-start.5) | copy-done | bytes 2097176
  35.2 0.0 copy-start.2
  35.2 0.0 copy-start.3
  35.2 0.0 copy-start.7
  35.2 11.2 %all-to-all-done = f32[16,1,128,128]{3,2,1,0:T(8,128)S(1)} async-done(((f32[16,1,128,128]{3,2,1,0:T(8,128)}), f32[16,1,128,128]{3,2,1,0:T(8,128)S(1)}, u32[]{:S(2)}, u32[]{:S(2)}) %all-to-all-start) | async-done | bytes 1048608 | tf_op jit(solution)/shard_map/all_to_all | solution.py:250
  46.5 0.0 copy-done.1
  46.5 0.8 %overlap.1 = f32[16,8,128]{2,1,0:T(8,128)} custom-call(f32[16,128,128]{2,1,0:T(8,128)S(1)} %bitcast.34, f32[16,128,128]{2,1,0:T(8,128)S(1)} %get-tuple-element.19.adjoint_ref, f32[8,128]{1,0:T(8,128)S(1)} %copy-done.1), custom_call_target="tpu_custom_call" | custom-call | tf_op jit(solution)/shard_map/overlap/pallas_call | solution.py:291
  47.3 6.8 %all-to-all-start.2 = ((f32[16,8,128]{2,1,0:T(8,128)}), f32[16,8,128]{2,1,0:T(8,128)S(1)}, u32[]{:S(2)}, u32[]{:S(2)}) async-start(f32[16,8,128]{2,1,0:T(8,128)} %overlap.1), calls=%async_computation.2 | async-start | bytes 131072 | tf_op jit(solution)/shard_map/all_to_all | solution.py:299
  54.1 0.0 copy-done.2
  54.1 0.0 copy-done.3
  54.1 0.0 copy-done.7
  54.1 0.0 copy-start.6
  54.1 1.6 %copy-done.6 = bf16[16,256,256]{2,1,0:T(8,128)(2,1)S(1)} copy-done((bf16[16,256,256]{2,1,0:T(8,128)(2,1)S(1)}, bf16[16,256,256]{2,1,0:T(8,128)(2,1)}, u32[]{:S(2)}) %copy-start.6) | copy-done | bytes 2097176
  55.7 0.0 copy-start.8
  55.7 1.0 %copy-done.8 = f32[8,128,128]{2,1,0:T(8,128)S(1)} copy-done((f32[8,128,128]{2,1,0:T(8,128)S(1)}, f32[8,128,128]{2,1,0:T(8,128)}, u32[]{:S(2)}) %copy-start.8) | copy-done | bytes 524312
  56.8 0.0 copy-start
  56.8 4.0 %remote_terms.1 = (f32[1024,128]{1,0:T(8,128)S(1)}, f32[1024,128]{1,0:T(8,128)}) custom-call(s32[1,2,16]{2,1,0:T(2,128)S(1)} %bitcast.41, s32[1,2,16]{2,1,0:T(2,128)S(1)} %bitcast.43, f32[16,128,128]{2,1,0:T(8,128)S(1)} %bitcast.35, f32[8,128,128]{2,1,0:T(8,128)S(1)} %copy-done.8, bf16[16,256,256]{2,1,0:T(8,128)(2,1)S(1)} %copy-done.6, ...), custom_call_target="tpu_custom_call" | custom-call | flops 4000000000 | bytes 6291456 | tf_op jit(solution)/shard_map/remote_terms/pallas_call | solution.py:301
  60.8 0.2 all-to-all-done.2.sums_ref
  61.0 0.0 copy-done
  61.0 1.0 %residual.1 = f32[1024,128]{1,0:T(8,128)} custom-call(f32[16,8,128]{2,1,0:T(8,128)S(1)} %all-to-all-done.2.sums_ref, f32[1024,128]{1,0:T(8,128)S(1)} %get-tuple-element.21.hpsi_rows, f32[1024,128]{1,0:T(8,128)S(1)} %bitcast.39), custom_call_target="tpu_custom_call" | custom-call | tf_op jit(solution)/shard_map/residual/pallas_call | solution.py:316
Async XLA Ops:
  6.2 13.7 %all-to-all-start.1 = ((s32[16,1,128]{2,1,0:T(1,128)}), s32[16,1,128]{2,1,0:T(1,128)S(1)}, u32[]{:S(2)}, u32[]{:S(2)}) async-start(s32[16,1,128]{2,1,0:T(1,128)} %get-tuple-element.15), calls=%async_computation.1 | async-start | bytes 16384 | tf_op jit(solution)/shard_map/all_to_all | solution.py:268
  19.9 26.6 %all-to-all-start = ((f32[16,1,128,128]{3,2,1,0:T(8,128)}), f32[16,1,128,128]{3,2,1,0:T(8,128)S(1)}, u32[]{:S(2)}, u32[]{:S(2)}) async-start(f32[16,1,128,128]{3,2,1,0:T(8,128)} %bitcast.44), calls=%async_computation | async-start | bytes 2097152 | tf_op jit(solution)/shard_map/all_to_all | solution.py:250
  23.6 6.4 %copy-start.4 = (bf16[16,128,512]{2,1,0:T(8,128)(2,1)S(1)}, bf16[16,128,512]{2,1,0:T(8,128)(2,1)}, u32[]{:S(2)}) copy-start(bf16[16,128,512]{2,1,0:T(8,128)(2,1)} %get-tuple-element.16.refs_2_) | copy-start | bytes 6291460
  30.0 16.5 %copy-start.1 = (f32[8,128]{1,0:T(8,128)S(1)}, f32[8,128]{1,0:T(8,128)}, u32[]{:S(2)}) copy-start(f32[8,128]{1,0:T(8,128)} %get-tuple-element.20.near_sums_ref) | copy-start | bytes 12292
  33.9 1.3 %copy-start.5 = (bf16[16,256,256]{2,1,0:T(8,128)(2,1)}, bf16[16,256,256]{2,1,0:T(8,128)(2,1)S(1)}, u32[]{:S(2)}) copy-start(bf16[16,256,256]{2,1,0:T(8,128)(2,1)S(1)} %get-tuple-element.17.lefts_ref) | copy-start | bytes 6291460
  35.2 18.9 %copy-start.2 = (s32[16,1,2]{0,2,1:T(2,128)S(1)}, s32[16,1,2]{0,2,1:T(2,128)}, u32[]{:S(2)}) copy-start(s32[16,1,2]{0,2,1:T(2,128)} %param.17) | copy-start | bytes 388
  35.2 18.9 %copy-start.3 = (s32[16,1,2]{0,2,1:T(2,128)S(1)}, s32[16,1,2]{0,2,1:T(2,128)}, u32[]{:S(2)}) copy-start(s32[16,1,2]{0,2,1:T(2,128)} %param.18) | copy-start | bytes 388
  35.2 18.9 %copy-start.7 = (bf16[16,128,256]{2,1,0:T(8,128)(2,1)S(1)}, bf16[16,128,256]{2,1,0:T(8,128)(2,1)}, u32[]{:S(2)}) copy-start(bf16[16,128,256]{2,1,0:T(8,128)(2,1)} %get-tuple-element.13.rights_ref) | copy-start | bytes 3145732
  47.3 13.7 %all-to-all-start.2 = ((f32[16,8,128]{2,1,0:T(8,128)}), f32[16,8,128]{2,1,0:T(8,128)S(1)}, u32[]{:S(2)}, u32[]{:S(2)}) async-start(f32[16,8,128]{2,1,0:T(8,128)} %overlap.1), calls=%async_computation.2 | async-start | bytes 131072 | tf_op jit(solution)/shard_map/all_to_all | solution.py:299
  54.1 1.6 %copy-start.6 = (bf16[16,256,256]{2,1,0:T(8,128)(2,1)S(1)}, bf16[16,256,256]{2,1,0:T(8,128)(2,1)}, u32[]{:S(2)}) copy-start(bf16[16,256,256]{2,1,0:T(8,128)(2,1)} %copy-done.5) | copy-start | bytes 6291460
  55.7 1.0 %copy-start.8 = (f32[8,128,128]{2,1,0:T(8,128)S(1)}, f32[8,128,128]{2,1,0:T(8,128)}, u32[]{:S(2)}) copy-start(f32[8,128,128]{2,1,0:T(8,128)} %get-tuple-element.14.near_ref) | copy-start | bytes 1572868
  56.8 4.2 %copy-start = (f32[8,16384]{1,0:T(8,128)S(1)}, f32[8,16384]{1,0:T(8,128)}, u32[]{:S(2)}) copy-start(f32[8,16384]{1,0:T(8,128)} %param.11) | copy-start | bytes 1572868
